TPU v7x, 32 devices: a whole 2x2x4 slice. The times are simulated.
32 devices in a mesh: seq: 4 (over y, x), ctx: 8 (over z, core).
Axes of the slice: x: 2, y: 2, z: 4, core: 2. Of those that a mesh axis runs over, the one named last changes fastest.
Arguments:
- tokens: bfloat16 [4, 2048, 768], P('seq', 'ctx'), may hold values from -6 to 6
- gain_one: float32 [768], replicated, may hold values from 0.5 to 1.5
- bias_one: float32 [768], replicated, may hold values from -1.75 to 1.75
- w_query: bfloat16 [768, 768], replicated, may hold values from -0.3125 to 0.3125
- w_key: bfloat16 [768, 768], replicated, may hold values from -0.3125 to 0.3125
- w_value: bfloat16 [768, 768], replicated, may hold values from -0.21875 to 0.21875
- w_out: bfloat16 [768, 768], replicated, may hold values from -0.875 to 0.875
- gain_two: float32 [768], replicated, may hold values from 0.5 to 1.5
- bias_two: float32 [768], replicated, may hold values from -1.75 to 1.75
- w_up: bfloat16 [768, 3072], replicated, may hold values from -0.21875 to 0.21875
- w_down: bfloat16 [3072, 768], replicated, may hold values from -0.109375 to 0.109375
- cotangent: bfloat16 [4, 2048, 768], P('seq', 'ctx'), may hold values from -6 to 6
- cluster_ids: int32 [4, 2048, 12], P('seq', 'ctx'), may hold values from 0 to 99, as said below
- top_keys: int32 [4, 12, 100, 32], P('seq'), may hold values from 0 to 2047, as said below
Outputs:
- output: float32 [4, 2048, 768], P('seq', 'ctx')
- input_grad: float32 [4, 2048, 768], P('seq', 'ctx')
- grad_gain_one: float32 [768], P('ctx')
- grad_bias_one: float32 [768], P('ctx')
- grad_query: float32 [768, 768], P('ctx')
- grad_key: float32 [768, 768], P('ctx')
- grad_value: float32 [768, 768], P('ctx')
- grad_out: float32 [768, 768], P('ctx')
- grad_gain_two: float32 [768], P('ctx')
- grad_bias_two: float32 [768], P('ctx')
- grad_up: float32 [768, 3072], P('ctx')
- down_weight_gradient: float32 [3072, 768], P('ctx')
Inputs may be any that keep to these rules, and one draw needn't show every extreme that they name: `cluster_ids`: every one of the 100 clusters of every head of every sequence holds one token or more. `top_keys`: the 32 positions of one cluster are distinct; the t-th lies in the t-th of 32 equal ranges of the sequence.
All inputs are finite; a program needn't handle non-finite values.
Results may differ from a plain program's by a relative error of at most 0.017.
Values may be sent and summed in bfloat16 or wider, within the bound.
No kernel may reach another device: no remote copies, remote signals or barrier semaphores. Data moves between devices by JAX's collectives and lax.ppermute only.
A program may use at most 192 MiB of HBM per device.

v0:
```python
import math

import jax
import jax.numpy as jnp
from jax import lax
from jax.sharding import PartitionSpec as P

EPS = 1e-05
HIGH = lax.Precision.HIGHEST


def layer_norm(values, gain, bias):
    center = values - jnp.mean(values, -1, keepdims=True)
    spread = jnp.mean(center * center, -1, keepdims=True)
    return center * lax.rsqrt(spread + EPS) * gain + bias


def project(left_side, weight_matrix):
    return jnp.einsum("jrb,bi->jri", left_side, weight_matrix, preferred_element_type=jnp.float32)


def project_back(gradient_value, weight_matrix):
    return jnp.einsum(
        "gyf,zf->gyz", gradient_value, weight_matrix, preferred_element_type=jnp.float32
    )


def weight_grad(left_side, gradient_value):
    return jnp.einsum("sli,slj->ij", left_side, gradient_value, preferred_element_type=jnp.float32)


def softmax_last(scores):
    shifted = jnp.exp(scores - jnp.max(scores, -1, keepdims=True))
    return shifted / jnp.sum(shifted, -1, keepdims=True)


def range_table(positions, full_len):
    chosen = positions.shape[2]
    stride = full_len // chosen
    offsets = positions - (jnp.arange(chosen, dtype=jnp.int32) * stride)[None, None, :]
    return (offsets[..., None] == jnp.arange(stride, dtype=jnp.int32)).astype(jnp.float32)


def pick_keys(dense, table):
    rows, heads, chosen, stride = table.shape
    return jnp.sum(dense.reshape(rows, heads, chosen, stride) * table, axis=-1)


def spread_keys(weights, table):
    rows, heads, chosen, stride = table.shape
    return (
        (weights.astype(jnp.float32)[..., None] * table)
        .reshape(rows, heads, chosen * stride)
        .astype(jnp.bfloat16)
    )


def per_device(
    tokens,
    gain_one,
    bias_one,
    w_query,
    w_key,
    w_value,
    w_out,
    gain_two,
    bias_two,
    w_up,
    w_down,
    cotangent,
    cluster_ids,
    top_keys,
):
    seq_count, local_len, width = tokens.shape
    heads = cluster_ids.shape[2]
    clusters = top_keys.shape[2]
    chosen = top_keys.shape[3]
    head_size = width // heads
    ctx_count = lax.axis_size("ctx")
    owner_index = lax.axis_index("ctx")
    full_len = local_len * ctx_count
    owner_count = (clusters + ctx_count - 1) // ctx_count
    slot_count = owner_count * ctx_count
    flat_rows = seq_count * heads * owner_count
    score_scale = 1.0 / math.sqrt(head_size)
    inputs = tokens.astype(jnp.float32)
    normed_one = layer_norm(inputs, gain_one, bias_one).astype(jnp.bfloat16)
    query = project(normed_one, w_query).astype(jnp.bfloat16)
    key = project(normed_one, w_key).astype(jnp.bfloat16)
    value = project(normed_one, w_value).astype(jnp.bfloat16)
    key_whole, value_whole = (
        lax.all_gather(key, "ctx", axis=1, tiled=True),
        lax.all_gather(value, "ctx", axis=1, tiled=True),
    )
    key_heads = key_whole.reshape(seq_count, full_len, heads, head_size)
    value_heads = value_whole.reshape(seq_count, full_len, heads, head_size)
    query_heads = query.reshape(seq_count, local_len, heads, head_size)
    onehot = (cluster_ids[..., None] == jnp.arange(slot_count)).astype(jnp.float32)
    onehot_low = onehot.astype(jnp.bfloat16)
    partial_value = jnp.einsum(
        "slhc,slhd->shcd", onehot_low, query_heads, preferred_element_type=jnp.float32
    )
    counts = jnp.sum(onehot, axis=1)
    cent_sum, cent_count = (
        lax.psum_scatter(partial_value, "ctx", scatter_dimension=2, tiled=True),
        lax.psum_scatter(counts, "ctx", scatter_dimension=2, tiled=True),
    )
    safe_count = jnp.maximum(cent_count, 1.0)
    centroid = (cent_sum / safe_count[..., None]).astype(jnp.bfloat16)
    stride = full_len // chosen
    filler = jnp.broadcast_to(
        jnp.arange(chosen) * stride, (seq_count, heads, slot_count - clusters, chosen)
    )
    padded_keys = jnp.concatenate([top_keys, filler], axis=2)
    my_keys = lax.dynamic_slice_in_dim(padded_keys, owner_index * owner_count, owner_count, 2)
    flat_keys = my_keys.reshape(flat_rows, chosen)
    cscore = score_scale * jnp.einsum(
        "shcd,slhd->shcl", centroid, key_heads, preferred_element_type=jnp.float32
    )
    cprob = softmax_last(cscore)
    cprob_low = cprob.astype(jnp.bfloat16)
    clear_top = jax.vmap(lambda line, index: line.at[index].set(0))
    rest_weights = clear_top(cprob_low.reshape(flat_rows, full_len), flat_keys).reshape(cprob.shape)
    rest_rows = jnp.einsum(
        "shcl,slhd->shcd", rest_weights, value_heads, preferred_element_type=jnp.float32
    ).astype(jnp.bfloat16)
    mass_rows = jnp.sum(jnp.take_along_axis(cprob, my_keys, axis=3), axis=3).astype(jnp.bfloat16)
    rest_all, mass_all = (
        lax.all_gather(rest_rows, "ctx", axis=2, tiled=True),
        lax.all_gather(mass_rows, "ctx", axis=2, tiled=True),
    )
    mass_tok = jnp.einsum("slhc,shc->slh", onehot_low, mass_all, preferred_element_type=jnp.float32)
    rest_tok = jnp.einsum(
        "slhc,shcd->slhd", onehot_low, rest_all, preferred_element_type=jnp.float32
    )
    head_pick = jnp.arange(heads)[None, :]
    entry = 0
    positions = padded_keys[entry][head_pick, cluster_ids[entry]]
    table = range_table(positions, full_len)
    dense_scores = jnp.einsum(
        "ihd,lhd->ihl", query_heads[entry], key_heads[entry], preferred_element_type=jnp.float32
    )
    mscore = score_scale * pick_keys(dense_scores, table)
    mprob = softmax_last(mscore)
    member = jnp.einsum(
        "ihl,lhd->ihd",
        spread_keys(mprob.astype(jnp.bfloat16), table),
        value_heads[entry],
        preferred_element_type=jnp.float32,
    )
    attended_list = [
        (mass_tok[entry][..., None] * member + rest_tok[entry]).reshape(local_len, width)
    ]
    member_list = [member]
    weight_list = [mprob]
    position_list = [positions]
    attended = jnp.stack(attended_list).astype(jnp.bfloat16)
    middle = inputs + project(attended, w_out)
    normed_two = layer_norm(middle, gain_two, bias_two).astype(jnp.bfloat16)
    upper = project(normed_two, w_up)
    active = jax.nn.gelu(upper).astype(jnp.bfloat16)
    output = middle + project(active, w_down)
    down_weight_gradient = weight_grad(active, cotangent)
    d_active = project_back(cotangent, w_down)
    gelu_pull = jax.vjp(jax.nn.gelu, upper)[1]
    d_upper = gelu_pull(d_active)[0].astype(jnp.bfloat16)
    grad_up = weight_grad(normed_two, d_upper)
    d_normed_two = project_back(d_upper, w_up)
    norm_two_pull = jax.vjp(layer_norm, middle, gain_two, bias_two)[1]
    d_mid_norm, grad_gain_two, grad_bias_two = norm_two_pull(d_normed_two)
    d_mid = cotangent.astype(jnp.float32) + d_mid_norm
    d_attn = d_mid.astype(jnp.bfloat16)
    grad_out = weight_grad(attended, d_attn)
    d_attended = project_back(d_attn, w_out).astype(jnp.bfloat16)
    d_att_heads = d_attended.reshape(seq_count, local_len, heads, head_size)
    key_back, value_back = (key_whole, value_whole)
    key_back_heads = key_back.reshape(seq_count, full_len, heads, head_size)
    value_back_heads = value_back.reshape(seq_count, full_len, heads, head_size)
    entry = 0
    table = range_table(position_list[entry], full_len)
    grad_heads = d_att_heads[entry].astype(jnp.float32)
    d_member = (mass_tok[entry][..., None] * grad_heads).astype(jnp.bfloat16)
    dmass_list = [jnp.sum(grad_heads * member_list[entry], axis=-1)]
    mprob = weight_list[entry]
    mprob_low = mprob.astype(jnp.bfloat16)
    dense_dp = jnp.einsum(
        "ihd,lhd->ihl", d_member, value_back_heads[entry], preferred_element_type=jnp.float32
    )
    d_weights = pick_keys(dense_dp, table)
    d_mscore = (mprob * (d_weights - jnp.sum(mprob * d_weights, -1, keepdims=True))).astype(
        jnp.bfloat16
    )
    spread_grad = spread_keys(d_mscore, table)
    dq_list = [
        score_scale
        * jnp.einsum(
            "ihl,lhd->ihd", spread_grad, key_back_heads[entry], preferred_element_type=jnp.float32
        ).reshape(local_len, width)
    ]
    dk_list = [
        score_scale
        * jnp.einsum(
            "ihl,ihd->lhd", spread_grad, query_heads[entry], preferred_element_type=jnp.float32
        ).reshape(full_len, width)
    ]
    dv_list = [
        jnp.einsum(
            "ihl,ihd->lhd",
            spread_keys(mprob_low, table),
            d_member,
            preferred_element_type=jnp.float32,
        ).reshape(full_len, width)
    ]
    dq_member = jnp.stack(dq_list)
    d_mass_tok = jnp.stack(dmass_list)
    d_rest_part = jnp.einsum(
        "slhc,slhd->shcd", onehot_low, d_att_heads, preferred_element_type=jnp.float32
    )
    d_mass_part = jnp.einsum("slhc,slh->shc", onehot, d_mass_tok, precision=HIGH)
    d_rest, d_mass = (
        lax.psum_scatter(d_rest_part, "ctx", scatter_dimension=2, tiled=True),
        lax.psum_scatter(d_mass_part, "ctx", scatter_dimension=2, tiled=True),
    )
    d_rest_low = d_rest.astype(jnp.bfloat16)
    d_cprob = jnp.einsum(
        "shcd,slhd->shcl", d_rest_low, value_back_heads, preferred_element_type=jnp.float32
    )
    assign_top_keys = jax.vmap(lambda line, index, update: line.at[index].set(update))
    mass_fill = jnp.broadcast_to(d_mass.reshape(flat_rows, 1), (flat_rows, chosen))
    d_cprob = assign_top_keys(d_cprob.reshape(flat_rows, full_len), flat_keys, mass_fill).reshape(
        cprob.shape
    )
    d_cscore = (cprob * (d_cprob - jnp.sum(cprob * d_cprob, -1, keepdims=True))).astype(
        jnp.bfloat16
    )
    d_centroid = score_scale * jnp.einsum(
        "shcl,slhd->shcd", d_cscore, key_back_heads, preferred_element_type=jnp.float32
    )
    d_csum = (d_centroid / safe_count[..., None]).astype(jnp.bfloat16)
    d_csum_all = lax.all_gather(d_csum, "ctx", axis=2, tiled=True)
    d_query = (
        dq_member
        + jnp.einsum(
            "slhc,shcd->slhd", onehot_low, d_csum_all, preferred_element_type=jnp.float32
        ).reshape(seq_count, local_len, width)
    ).astype(jnp.bfloat16)
    dk_cent = score_scale * jnp.einsum(
        "shcl,shcd->slhd", d_cscore, centroid, preferred_element_type=jnp.float32
    )
    dv_cent = jnp.einsum(
        "shcl,shcd->slhd", rest_weights, d_rest_low, preferred_element_type=jnp.float32
    )
    dk_part = jnp.stack(dk_list) + dk_cent.reshape(seq_count, full_len, width)
    dv_part = jnp.stack(dv_list) + dv_cent.reshape(seq_count, full_len, width)
    d_key, d_value = (
        lax.psum_scatter(dk_part, "ctx", scatter_dimension=1, tiled=True),
        lax.psum_scatter(dv_part, "ctx", scatter_dimension=1, tiled=True),
    )
    d_key = d_key.astype(jnp.bfloat16)
    d_value = d_value.astype(jnp.bfloat16)
    grad_query = weight_grad(normed_one, d_query)
    grad_key = weight_grad(normed_one, d_key)
    grad_value = weight_grad(normed_one, d_value)
    d_normed_one = (
        project_back(d_query, w_query) + project_back(d_key, w_key) + project_back(d_value, w_value)
    )
    norm_one_pull = jax.vjp(layer_norm, inputs, gain_one, bias_one)[1]
    d_in_norm, grad_gain_one, grad_bias_one = norm_one_pull(d_normed_one)
    input_grad = d_mid + d_in_norm
    summed = (
        lax.psum_scatter(grad_gain_one, "ctx", scatter_dimension=0, tiled=True),
        lax.psum_scatter(grad_bias_one, "ctx", scatter_dimension=0, tiled=True),
        lax.psum_scatter(grad_query, "ctx", scatter_dimension=0, tiled=True),
        lax.psum_scatter(grad_key, "ctx", scatter_dimension=0, tiled=True),
        lax.psum_scatter(grad_value, "ctx", scatter_dimension=0, tiled=True),
        lax.psum_scatter(grad_out, "ctx", scatter_dimension=0, tiled=True),
        lax.psum_scatter(grad_gain_two, "ctx", scatter_dimension=0, tiled=True),
        lax.psum_scatter(grad_bias_two, "ctx", scatter_dimension=0, tiled=True),
        lax.psum_scatter(grad_up, "ctx", scatter_dimension=0, tiled=True),
        lax.psum_scatter(down_weight_gradient, "ctx", scatter_dimension=0, tiled=True),
    )
    summed = lax.psum(
        (
            summed[0],
            summed[1],
            summed[2],
            summed[3],
            summed[4],
            summed[5],
            summed[6],
            summed[7],
            summed[8],
            summed[9],
        ),
        "seq",
    )
    return (
        output,
        input_grad,
        summed[0],
        summed[1],
        summed[2],
        summed[3],
        summed[4],
        summed[5],
        summed[6],
        summed[7],
        summed[8],
        summed[9],
    )


def solution(mesh):
    in_specs = (
        P("seq", "ctx", None),
        P(),
        P(),
        P(),
        P(),
        P(),
        P(),
        P(),
        P(),
        P(),
        P(),
        P("seq", "ctx", None),
        P("seq", "ctx", None),
        P("seq", None, None, None),
    )
    out_specs = (
        P("seq", "ctx", None),
        P("seq", "ctx", None),
        P("ctx"),
        P("ctx"),
        P("ctx", None),
        P("ctx", None),
        P("ctx", None),
        P("ctx", None),
        P("ctx"),
        P("ctx"),
        P("ctx", None),
        P("ctx", None),
    )
    return jax.shard_map(
        per_device, mesh=mesh, in_specs=in_specs, out_specs=out_specs, check_vma=False
    )
```

profile of v0, /device:TPU:0, one launch (start us, length us, event | category | flops | bytes accessed | tf_op | source)
XLA Modules:
  0.0 1044.6 jit_solution(8632469210238871567)
XLA Ops:
  11.1 2.7 convolution_convert_fusion.3
  16.1 2.0 copy.160
  19.7 2.6 convolution_convert_fusion.1
  24.7 31.0 %all-reduce.1 = f32[1,12,104]{1,0,2:T(1,128)S(1)} all-reduce(f32[1,12,104]{1,0,2:T(1,128)S(1)} %copy.161), channel_id=8, replica_groups=mesh['seq'=4,'ctx'=8] {'ctx'}, use_global_device_ids=true, to_apply=%region_4.0.clone | all-reduce | flops 1248 | bytes 9984
  57.3 33.6 %gather_fusion = s32[3072,32]{1,0:T(8,128)} fusion(s32[12,104,32]{2,1,0:T(8,128)S(1)} %bitcast.231, s32[3072]{0:T(1024)S(1)} %reshape.626), kind=kCustom, calls=%fused_computation | custom fusion | bytes 811008 | tf_op jit(solution)/shard_map/gather | solution.py:138
  91.0 2.6 reshape.629
  93.6 3.1 broadcast_subtract_fusion
  96.7 2.3 copy.170
  100.0 17.5 %all-gather.9.cloned.1.call-done = bf16[2048,768]{1,0:T(8,128)(2,1)} async-done(((bf16[256,768]{1,0:T(8,128)(2,1)}), bf16[2048,768]{1,0:T(8,128)(2,1)}) %all-gather.9.cloned.1.call-update) | async-done | bytes 3145744 | tf_op jit(solution)/shard_map/all_gather | solution.py:92
  117.5 4.7 copy.164
  122.2 7.7 select_reduce_fusion.1
  129.9 4.0 fusion.127
  133.9 2.6 fusion.123
  138.1 47.6 %gather_fusion.1 = f32[4992]{0:T(1024)S(1)} fusion(f32[12,13,2048]{2,1,0:T(8,128)S(1)} %get-tuple-element.35, s32[4992]{0:T(1024)S(1)} %reshape.634), kind=kCustom, calls=%fused_computation.1 | custom fusion | bytes 99840 | tf_op jit(solution)/shard_map/jit(take_along_axis)/gather | solution.py:127
  187.5 14.0 %all-gather.5 = bf16[8,13,12]{2,1,0:T(8,128)(2,1)S(1)} all-gather(bf16[1,13,12]{2,1,0:T(8,128)(2,1)S(1)} %bitcast.264), channel_id=3, replica_groups=mesh['seq'=4,'ctx'=8] {'ctx'}, dimensions={0}, use_global_device_ids=true | all-gather | bytes 2808 | tf_op jit(solution)/shard_map/all_gather | solution.py:130
  203.2 41.5 %scatter_fusion = bf16[319488]{0:T(1024)(128)(2,1)S(1)} fusion(bf16[319488]{0:T(1024)(128)(2,1)S(1)} %reshape.615, s32[4992]{0:T(1024)S(1)} %reshape.640, bf16[4992]{0:T(1024)(128)(2,1)S(1)} %broadcast.355), kind=kCustom, calls=%fused_computation.2 | custom fusion | bytes 49920
  246.1 1.9 fusion.124
  248.0 4.7 copy.167
  252.7 3.1 convolution_convert_fusion.4
  255.8 15.6 %all-gather.3 = bf16[12,104,64]{2,0,1:T(8,128)(2,1)} all-gather(bf16[12,13,64]{2,0,1:T(8,128)(2,1)S(1)} %copy.174), channel_id=5, replica_groups=mesh['seq'=4,'ctx'=8] {'ctx'}, dimensions={1}, use_global_device_ids=true | all-gather | bytes 179712 | tf_op jit(solution)/shard_map/all_gather | solution.py:129
  271.4 7.7 fusion.5
  279.2 7.7 convolution_bitcast_fusion.3
  288.7 4.6 fusion.113
  293.4 3.1 fusion.12
  296.5 2.2 fusion.50
  303.4 11.1 %fusion.76 = f32[12,64,2048]{2,1,0:T(8,128)} fusion(bf16[256,12,2048]{0,2,1:T(8,128)(2,1)} %fusion.5, bf16[256,12,64]{0,2,1:T(8,128)(2,1)S(1)} %bitcast.240, f32[256,12]{0,1:T(8,128)} %bitcast.257), kind=kOutput, calls=%fused_computation.130 | convolution fusion | flops 805896192 | bytes 19279872 | tf_op jit(solution)/shard_map/ihl,ihd->lhd/dot_general | solution.py:207
  318.4 2.0 copy.178
  320.4 105.4 %all-reduce.19 = (bf16[1,12,104,64]{3,0,1,2:T(2,128)(2,1)}, f32[1,12,104]{1,0,2:T(1,128)}) all-reduce(f32[1,12,104,64]{3,0,1,2:T(1,128)} %copy.178, f32[1,12,104]{1,0,2:T(1,128)} %bitcast.260), channel_id=9, replica_groups=mesh['seq'=4,'ctx'=8] {'ctx'}, use_global_device_ids=true, to_apply=%region_18.19.clone | all-reduce | flops 81120 | bytes 489216
  427.8 1.8 copy-done.6
  429.6 3.7 bitcast_add_fusion
  434.0 7.2 select_reduce_fusion
  441.2 1.7 fusion.95
  442.9 2.5 reshape.619
  446.5 26.9 %scatter_fusion.1 = f32[319488]{0:T(1024)} fusion(f32[319488]{0:T(1024)} %reshape.619, s32[4992]{0:T(1024)S(1)} %copy-done.31, f32[4992]{0:T(1024)S(1)} %reshape.648), kind=kCustom, calls=%fused_computation.3 | custom fusion | bytes 79872
  473.4 2.5 reshape.607
  476.1 7.7 fusion.4
  483.8 1.8 multiply_reduce_fusion
  486.1 1.8 convolution_multiply_fusion.1
  487.9 11.3 %convolution_multiply_fusion = f32[12,64,2048]{2,1,0:T(8,128)} fusion(bf16[256,12,64]{0,2,1:T(8,128)(2,1)S(1)} %bitcast.248, bf16[256,12,2048]{0,2,1:T(8,128)(2,1)} %fusion.4), kind=kOutput, calls=%fused_computation.20 | convolution fusion | flops 806879232 | bytes 19267584 | tf_op jit(solution)/shard_map/ihl,ihd->lhd/dot_general | solution.py:202
  499.2 7.4 bitcast_add_fusion.1
  507.7 1.9 fusion.132
  509.7 3.0 fusion.38
  512.7 16.0 %all-gather.4 = bf16[12,104,64]{2,0,1:T(8,128)(2,1)S(1)} all-gather(bf16[12,13,64]{2,0,1:T(8,128)(2,1)S(1)} %copy.181), channel_id=6, replica_groups=mesh['seq'=4,'ctx'=8] {'ctx'}, dimensions={1}, use_global_device_ids=true | all-gather | bytes 179712 | tf_op jit(solution)/shard_map/all_gather | solution.py:240
  529.1 7.0 fusion.48
  536.1 2.2 fusion.117
  538.4 3.2 fusion.62
  541.7 38.7 %reduce-scatter.9.cloned.1.call-done = f32[1,256,768]{1,2,0:T(8,128)} async-done(((f32[1,2048,768]{1,2,0:T(8,128)}), f32[1,256,768]{1,2,0:T(8,128)}) %reduce-scatter.9.cloned.1.call-update) | async-done | bytes 786448 | tf_op jit(solution)/shard_map/reduce_scatter | solution.py:256
  580.4 3.2 fusion.65
  583.7 7.8 fusion.68
  592.6 6.6 fusion.111
  599.6 17.4 %reduce-scatter.19.cloned.1.call-done = f32[96,768]{1,0:T(8,128)} async-done(((f32[768,768]{1,0:T(8,128)}), f32[96,768]{1,0:T(8,128)}) %reduce-scatter.19.cloned.1.call-update) | async-done | bytes 294928 | tf_op jit(solution)/shard_map/reduce_scatter | solution.py:276
  617.0 37.9 %reduce-scatter.13.cloned.1.call-done = f32[96,768]{1,0:T(8,128)} async-done(((f32[768,768]{1,0:T(8,128)}), f32[96,768]{1,0:T(8,128)}) %reduce-scatter.13.cloned.1.call-update) | async-done | bytes 294928 | tf_op jit(solution)/shard_map/reduce_scatter | solution.py:273
  654.9 37.7 %reduce-scatter.17.cloned.1.call-done = f32[96,768]{1,0:T(8,128)} async-done(((f32[768,768]{1,0:T(8,128)}), f32[96,768]{1,0:T(8,128)}) %reduce-scatter.17.cloned.1.call-update) | async-done | bytes 294928 | tf_op jit(solution)/shard_map/reduce_scatter | solution.py:275
  692.6 37.8 %reduce-scatter.15.cloned.1.call-done = f32[96,768]{1,0:T(8,128)} async-done(((f32[768,768]{1,0:T(8,128)}), f32[96,768]{1,0:T(8,128)}) %reduce-scatter.15.cloned.1.call-update) | async-done | bytes 294928 | tf_op jit(solution)/shard_map/reduce_scatter | solution.py:274
  730.4 100.9 %reduce-scatter.23.cloned.1.call-done = f32[384,768]{1,0:T(8,128)} async-done(((f32[3072,768]{1,0:T(8,128)}), f32[384,768]{1,0:T(8,128)}) %reduce-scatter.23.cloned.1.call-update) | async-done | bytes 1179664 | tf_op jit(solution)/shard_map/reduce_scatter | solution.py:280
  831.3 100.2 %reduce-scatter.21.cloned.1.call-done = f32[96,3072]{1,0:T(8,128)} async-done(((f32[768,3072]{1,0:T(8,128)}), f32[96,3072]{1,0:T(8,128)}) %reduce-scatter.21.cloned.1.call-update) | async-done | bytes 1179664 | tf_op jit(solution)/shard_map/reduce_scatter | solution.py:279
  933.5 1.9 fusion.131
  935.7 5.3 fusion.22
  943.8 26.0 %all-reduce.8 = (f32[768]{0:T(1024)S(1)}, f32[768]{0:T(1024)S(1)}, f32[768]{0:T(1024)S(1)}, f32[768]{0:T(1024)S(1)}) all-reduce(f32[768]{0:T(1024)S(1)} %get-tuple-element.14, f32[768]{0:T(1024)S(1)} %reduce_sum.219, f32[768]{0:T(1024)S(1)} %copy-done.74, f32[768]{0:T(1024)S(1)} %reduce_sum.224), channel_id=13, replica_groups=mesh['seq'=4,'ctx'=8] {'ctx'}, use_global_device_ids=true, to_apply=%region_28.29.clone | all-reduce | flops 3072 | bytes 24576
  970.0 10.7 %all-reduce.10 = (f32[96]{0:T(128)}, f32[96]{0:T(128)}, f32[96]{0:T(128)}, f32[96]{0:T(128)}) all-reduce(f32[96]{0:T(128)S(1)} %dynamic-slice.9, f32[96]{0:T(128)S(1)} %dynamic-slice.11, f32[96]{0:T(128)S(1)} %dynamic-slice.13, f32[96]{0:T(128)S(1)} %dynamic-slice.15), channel_id=1, replica_groups=mesh['seq'=4,'ctx'=8] {'seq'}, use_global_device_ids=true, to_apply=%region_29.30 | all-reduce | flops 384 | bytes 3072 | tf_op jit(solution)/shard_map/psum | solution.py:282
  981.9 46.6 %all-reduce.18.cloned.1.call-done = (f32[96,768]{1,0:T(8,128)}, f32[96,768]{1,0:T(8,128)}, f32[96,768]{1,0:T(8,128)}, f32[96,768]{1,0:T(8,128)}, f32[96,3072]{1,0:T(8,128)}, /*index=5*/f32[384,768]{1,0:T(8,128)}) async-done(((f32[96,768]{1,0:T(8,128)}, f32[96,768]{1,0:T(8,128)}, f32[96,768]{1,0:T(8,128)}, f32[96,768]{1,0:T(8,128)}, f32[96,3072]{1,0:T(8,128)}, /*index=5*/f32[384,768]{1,0:T(8,128)}), ...) | async-done | bytes 3538960 | tf_op jit(solution)/shard_map/psum | solution.py:282
  1028.6 1.8 copy.235
  1030.4 1.7 copy.236
  1032.1 1.7 copy.237
  (280 shorter events, 45.4 us)
Async XLA Ops:
  7.2 280.6 %copy-start = (bf16[768,768]{1,0:T(8,128)(2,1)S(1)}, bf16[768,768]{1,0:T(8,128)(2,1)}, u32[]{:S(2)}) copy-start(bf16[768,768]{1,0:T(8,128)(2,1)} %param.20) | copy-start | bytes 3538948
  7.2 91.8 %all-reduce.16.cloned.1.call-start = ((), (), s32[]{:S(2)}) async-start(), calls=%async_computation.18 | async-start | bytes 1277952
  8.5 11.2 %copy-start.59 = (f32[256]{0:T(256)}, f32[256]{0:T(256)S(1)}, u32[]{:S(2)}) copy-start(f32[256]{0:T(256)S(1)} %broadcast_multiply_fusion.1) | copy-start | bytes 3076
  8.5 9.7 copy-start.4
  8.5 9.7 copy-start.34
  8.5 9.7 copy-start.49
  8.5 9.7 copy-start.64
  10.4 9.3 copy-start.61
  11.1 11.9 %copy-start.44 = (s32[1,256,12]{1,2,0:T(8,128)}, s32[1,256,12]{1,2,0:T(8,128)S(1)}, u32[]{:S(2)}) copy-start(s32[1,256,12]{1,2,0:T(8,128)S(1)} %copy.221) | copy-start | bytes 36868
  15.0 107.2 %copy-start.23 = (bf16[256,768]{0,1:T(8,128)(2,1)}, bf16[256,768]{0,1:T(8,128)(2,1)S(1)}, u32[]{:S(2)}) copy-start(bf16[256,768]{0,1:T(8,128)(2,1)S(1)} %copy.159) | copy-start | bytes 1179652
  18.1 5.3 copy-start.77
  18.1 37.7 %copy-start.63 = (s32[1,256,12]{1,0,2:T(1,128)S(1)}, s32[1,256,12]{1,0,2:T(1,128)}, u32[]{:S(2)}) copy-start(s32[1,256,12]{1,0,2:T(1,128)} %param.26) | copy-start | bytes 36868
  18.1 38.0 %copy-start.48 = (s32[1,12,100,32]{2,3,1,0:T(8,128)S(1)}, s32[1,12,100,32]{2,3,1,0:T(8,128)}, u32[]{:S(2)}) copy-start(s32[1,12,100,32]{2,3,1,0:T(8,128)} %param.27) | copy-start | bytes 460804
  18.2 99.4 %all-gather.9.cloned.1.call-start = ((), (), s32[]{:S(2)}) async-start(), calls=%async_computation.16 | async-start | bytes 3538944 | tf_op jit(solution)/shard_map/all_gather | solution.py:92
  19.6 37.4 %copy-start.76 = (s32[2]{0:T(128)S(1)}, s32[2]{0:T(128)}, u32[]{:S(2)}) copy-start(s32[2]{0:T(128)} %constant.82) | copy-start | bytes 28
  19.6 37.4 %copy-start.75 = (s32[2]{0:T(128)S(1)}, s32[2]{0:T(128)}, u32[]{:S(2)}) copy-start(s32[2]{0:T(128)} %constant.85) | copy-start | bytes 28
  19.6 228.4 %all-gather.11.cloned.1.call-start = ((), (), s32[]{:S(2)}) async-start(), calls=%async_computation.17 | async-start | bytes 3538944 | tf_op jit(solution)/shard_map/all_gather | solution.py:93
  22.3 516.1 %reduce-scatter.11.cloned.1.call-start = ((), (), s32[]{:S(2)}) async-start(), calls=%async_computation.9 | async-start | bytes 7077888 | tf_op jit(solution)/shard_map/reduce_scatter | solution.py:257
  57.3 145.9 %copy-start.30 = (s32[4992]{0:T(1024)}, s32[4992]{0:T(1024)S(1)}, u32[]{:S(2)}) copy-start(s32[4992]{0:T(1024)S(1)} %reshape.640) | copy-start | bytes 59908
  99.0 23.3 %copy-start.10 = (s32[256,12,32]{0,2,1:T(8,128)}, s32[256,12,32]{0,2,1:T(8,128)S(1)}, u32[]{:S(2)}) copy-start(s32[256,12,32]{0,2,1:T(8,128)S(1)} %copy.170) | copy-start | bytes 1179652
  99.0 31.0 %copy-start.51 = (f32[12,13]{1,0:T(8,128)}, f32[12,13]{1,0:T(8,128)S(1)}, u32[]{:S(2)}) copy-start(f32[12,13]{1,0:T(8,128)S(1)} %maximum_bitcast_fusion) | copy-start | bytes 1876
  100.0 29.9 %copy-start.39 = (f32[1,12,13,64]{3,0,1,2:T(1,128)}, f32[1,12,13,64]{3,0,1,2:T(1,128)S(1)}, u32[]{:S(2)}) copy-start(f32[1,12,13,64]{3,0,1,2:T(1,128)S(1)} %constant_dynamic-slice_fusion.3) | copy-start | bytes 119812
  252.7 18.7 %copy-start.11 = (s32[256,12,32]{0,2,1:T(8,128)S(1)}, s32[256,12,32]{0,2,1:T(8,128)}, u32[]{:S(2)}) copy-start(s32[256,12,32]{0,2,1:T(8,128)} %copy-done.10) | copy-start | bytes 1179652
  252.7 18.7 %copy-start.55 = (s32[2048]{0:T(1024)S(1)}, s32[2048]{0:T(1024)}, u32[]{:S(2)}) copy-start(s32[2048]{0:T(1024)} %eq.79) | copy-start | bytes 24580
  279.1 7.7 copy-start.33
  279.2 7.8 copy-start.45
  279.2 7.8 copy-start.46
  279.2 8.6 copy-start.5
  287.8 5.6 slice-start.2
  288.4 10.4 copy-start.8
  288.4 10.4 copy-start.66
  288.6 10.1 copy-start.68
  288.7 4.7 copy-start.25
  288.7 4.7 slice-start.3
  288.7 7.8 slice-start
  293.3 3.1 copy-start.17
  293.4 3.2 slice-start.1
  303.4 11.2 %copy-start.13 = (f32[256,12,64]{0,2,1:T(8,128)S(1)}, f32[256,12,64]{0,2,1:T(8,128)}, u32[]{:S(2)}) copy-start(f32[256,12,64]{0,2,1:T(8,128)} %copy-done.12) | copy-start | bytes 2359300
  314.6 112.1 %copy-start.16 = (bf16[12,13,2048]{2,1,0:T(8,128)(2,1)S(1)}, bf16[12,13,2048]{2,1,0:T(8,128)(2,1)}, u32[]{:S(2)}) copy-start(bf16[12,13,2048]{2,1,0:T(8,128)(2,1)} %reshape.599) | copy-start | bytes 1916932
  433.3 7.9 copy-start.42
  433.3 147.1 %reduce-scatter.9.cloned.1.call-start = ((), (), s32[]{:S(2)}) async-start(), calls=%async_computation.8 | async-start | bytes 7077888 | tf_op jit(solution)/shard_map/reduce_scatter | solution.py:256
  434.0 7.2 copy-start.3
  441.2 5.3 copy-start.31
  446.5 29.4 %copy-start.43 = (f32[256,12,32]{0,2,1:T(8,128)S(1)}, f32[256,12,32]{0,2,1:T(8,128)}, u32[]{:S(2)}) copy-start(f32[256,12,32]{0,2,1:T(8,128)} %get-tuple-element.39) | copy-start | bytes 1179652
  506.6 110.4 %reduce-scatter.19.cloned.1.call-start = ((), (), s32[]{:S(2)}) async-start(), calls=%async_computation.13 | async-start | bytes 2654208 | tf_op jit(solution)/shard_map/reduce_scatter | solution.py:276
  509.7 145.2 %reduce-scatter.13.cloned.1.call-start = ((), (), s32[]{:S(2)}) async-start(), calls=%async_computation.10 | async-start | bytes 2654208 | tf_op jit(solution)/shard_map/reduce_scatter | solution.py:273
  509.7 19.3 %copy-start.2 = (bf16[2048,768]{0,1:T(8,128)(2,1)S(1)}, bf16[2048,768]{0,1:T(8,128)(2,1)}, u32[]{:S(2)}) copy-start(bf16[2048,768]{0,1:T(8,128)(2,1)} %copy.164) | copy-start | bytes 9437188
  529.0 7.1 copy-start.50
  529.0 7.1 copy-start.60
  529.1 7.1 copy-start.62
  529.1 7.1 copy-start.65
  538.3 154.2 %reduce-scatter.17.cloned.1.call-start = ((), (), s32[]{:S(2)}) async-start(), calls=%async_computation.12 | async-start | bytes 2654208 | tf_op jit(solution)/shard_map/reduce_scatter | solution.py:275
  541.6 42.1 %copy-start.26 = (bf16[1,256,768]{2,1,0:T(8,128)(2,1)S(1)}, bf16[1,256,768]{2,1,0:T(8,128)(2,1)}, u32[]{:S(2)}) copy-start(bf16[1,256,768]{2,1,0:T(8,128)(2,1)} %param.25) | copy-start | bytes 1179652
  541.7 188.8 %reduce-scatter.15.cloned.1.call-start = ((), (), s32[]{:S(2)}) async-start(), calls=%async_computation.11 | async-start | bytes 2654208 | tf_op jit(solution)/shard_map/reduce_scatter | solution.py:274
  583.6 247.7 %reduce-scatter.23.cloned.1.call-start = ((), (), s32[]{:S(2)}) async-start(), calls=%async_computation.15 | async-start | bytes 10616832 | tf_op jit(solution)/shard_map/reduce_scatter | solution.py:280
  591.5 340.0 %reduce-scatter.21.cloned.1.call-start = ((), (), s32[]{:S(2)}) async-start(), calls=%async_computation.14 | async-start | bytes 10616832 | tf_op jit(solution)/shard_map/reduce_scatter | solution.py:279
  599.3 429.3 %all-reduce.18.cloned.1.call-start = ((), (), s32[]{:S(2)}) async-start(), calls=%async_computation.19 | async-start | bytes 7077888 | tf_op jit(solution)/shard_map/psum | solution.py:282
  935.7 5.3 copy-start.27
  935.7 5.3 copy-start.35
  942.5 38.1 %copy-start.15 = (f32[1,256,768]{2,1,0:T(8,128)S(1)}, f32[1,256,768]{2,1,0:T(8,128)}, u32[]{:S(2)}) copy-start(f32[1,256,768]{2,1,0:T(8,128)} %copy-done.14) | copy-start | bytes 2359300
  942.5 38.1 %copy-start.73 = (f32[256]{0:T(256)S(1)}, f32[256]{0:T(256)}, u32[]{:S(2)}) copy-start(f32[256]{0:T(256)} %copy-done.72) | copy-start | bytes 3076
  1028.6 6.9 copy-start.37
  1028.6 7.9 copy-start.36
  1028.6 9.0 copy-start.1
  (30 other events, 42.1 us)
Sparse Core Ops, SparseCore 0:
  18.2 59.3 all-reduce.15
  79.9 37.6 all-gather.8
  119.7 37.1 all-gather.10
  433.4 70.2 reduce-scatter.10
  506.7 73.6 reduce-scatter.8
  582.6 34.3 reduce-scatter.18
  619.3 35.5 reduce-scatter.12
  657.2 35.3 reduce-scatter.16
  694.9 35.4 reduce-scatter.14
  732.6 98.7 reduce-scatter.22
  833.6 97.8 reduce-scatter.20
  935.2 93.3 all-reduce.17
where the time goes:
time: 1050 us; the launch traced here: 1040 us
  waiting for transfers between devices  435 us (41%)
  blocking collectives  219 us (21%)
  local copies, waits for them, and re-layouts  205 us (20%)
  matrix products  123 us (12%)
  other arithmetic  44.6 us (4%)
  between operations  16.9 us (2%)
    unnamed x3, blocking collectives  162 us
    reduce_scatter x1, waiting for transfers between devices, per_device(): lax.psum_scatter(down_weight_gradient, 'ctx', scatter_dimension=0, tiled=...  101 us
    reduce_scatter x1, waiting for transfers between devices, per_device(): lax.psum_scatter(grad_up, 'ctx', scatter_dimension=0, tiled=True)  100 us
    unnamed x191, local copies, waits for them, and re-layouts  94.7 us
    gather x3, local copies, waits for them, and re-layouts, per_device(): jnp.take_along_axis(cprob, my_keys, axis=3)  48.4 us
    psum x1, waiting for transfers between devices, per_device(): lax.psum((summed[0], summed[1], summed[2], summed[3], summed[4], summed[5...  46.6 us
    reduce_scatter x1, waiting for transfers between devices, per_device(): lax.psum_scatter(dk_part, 'ctx', scatter_dimension=1, tiled=True)  38.7 us
    reduce_scatter x1, waiting for transfers between devices, per_device(): lax.psum_scatter(grad_query, 'ctx', scatter_dimension=0, tiled=True)  37.9 us
  transfers between devices with their start and end apart: 12, of which 9 were waited for; matrix products, arithmetic and copies ran while one was open for 27% of the time, Pallas kernels for 0%

commit v1 on v0

v1 whole, which is shorter than its diff:
```python
import functools
import math

import jax
import jax.numpy as jnp
import numpy as np
from jax import lax
from jax.experimental import pallas as pl
from jax.experimental.pallas import tpu as pltpu
from jax.sharding import PartitionSpec as P

EPS = 1e-05
NEG = -1e30
F32 = jnp.float32
BF = jnp.bfloat16
VMEM_BYTES = 52 * 1024 * 1024


def dot(a, b):
    return lax.dot_general(a, b, (((1,), (0,)), ((), ())), preferred_element_type=F32)


def dot_nt(a, b):
    return lax.dot_general(a, b, (((1,), (1,)), ((), ())), preferred_element_type=F32)


def dot_tn(a, b):
    return lax.dot_general(a, b, (((0,), (0,)), ((), ())), preferred_element_type=F32)


def low_half():
    return lax.broadcasted_iota(jnp.int32, (1, 128), 1) < 64


def norm_parts(x):
    center = x - jnp.mean(x, -1, keepdims=True)
    spread = jnp.mean(center * center, -1, keepdims=True)
    rstd = lax.rsqrt(spread + EPS)
    return center * rstd, rstd


def norm_back(d_normed, xhat, rstd, gain):
    d_hat = d_normed * gain
    first = jnp.mean(d_hat, -1, keepdims=True)
    second = jnp.mean(d_hat * xhat, -1, keepdims=True)
    return rstd * (d_hat - first - xhat * second)


def rows_at(index, size):
    return pl.ds(pl.multiple_of(index * size, size), size)


def call(body, grid, in_specs, out_specs, out_shape, scratch=(), aliases=None, flops=0, moved=0):
    return pl.pallas_call(
        body,
        grid_spec=pltpu.PrefetchScalarGridSpec(
            num_scalar_prefetch=1,
            grid=grid,
            in_specs=in_specs,
            out_specs=out_specs,
            scratch_shapes=list(scratch),
        ),
        out_shape=out_shape,
        input_output_aliases=aliases or {},
        compiler_params=pltpu.CompilerParams(
            vmem_limit_bytes=VMEM_BYTES, dimension_semantics=("arbitrary",) * len(grid)
        ),
        cost_estimate=pl.CostEstimate(flops=flops, bytes_accessed=moved, transcendentals=0),
    )


def full(shape):
    return pl.BlockSpec(shape, lambda *_: (0,) * len(shape))


ANY = pl.BlockSpec(memory_space=pl.ANY)


def qkv_body(first, info, xa, xb, gain, bias, wq, wk, wv, *rest):
    outs = rest if first else rest[3:]
    core = info[0]
    block = xa.shape[0]
    for rel, ref in enumerate((xa, xb)):
        rows = rows_at(core ^ rel, block)
        xhat, _ = norm_parts(ref[...].astype(F32))
        normed = (xhat * gain[...] + bias[...]).astype(BF)
        for weight, out in ((wq, outs[0]), (wk, outs[1]), (wv, outs[2])):
            out[rows, :] = dot(normed, weight[...]).astype(BF)
        if first:
            outs[3][rows, :] = normed


def qkv_call(info, xa, xb, gain, bias, wq, wk, wv, full_len, previous):
    block, width = xa.shape
    half = width // 2
    first = previous is None
    weight = pl.BlockSpec((width, half), lambda i, s: (0, s[0]))
    into = pl.BlockSpec((2 * block, half), lambda i, s: (s[1], 0))
    shape = jax.ShapeDtypeStruct((full_len, half), BF)
    in_specs = [full((block, width))] * 2 + [full((1, width))] * 2 + [weight] * 3
    out_specs, out_shape = [into] * 3, [shape] * 3
    operands = [xa, xb, gain, bias, wq, wk, wv]
    aliases = None
    if first:
        out_specs.append(full((2 * block, width)))
        out_shape.append(jax.ShapeDtypeStruct((2 * block, width), BF))
    else:
        in_specs += [ANY] * 3
        operands += list(previous)
        aliases = {8: 0, 9: 1, 10: 2}
    return call(
        functools.partial(qkv_body, first),
        (1,),
        in_specs,
        out_specs,
        out_shape,
        aliases=aliases,
        flops=12 * block * width * half,
        moved=6 * width * half,
    )(info, *operands)


def top_mask(offs, expand, omod):
    return dot(offs, expand) == omod


def fwd_body(scale, tile, info, ids, ids_own, offs, expand, omod, q_all, k_all, v_all, q_own,
             att, mem, prob, lse, rm, cen, cst):
    keys, values, queries = k_all[...], v_all[...], q_all[...]
    full_len = keys.shape[0]
    rows = offs.shape[2]
    own = q_own.shape[0]
    lo = low_half()
    lane = lax.broadcasted_iota(jnp.int32, (1, 128), 1)
    cluster = lax.broadcasted_iota(jnp.int32, (rows, full_len), 0)
    hits = [cluster == ids[0, e : e + 1, :] for e in range(2)]
    hot = [jnp.where(h, 1.0, 0.0) for h in hits]
    counts = [jnp.sum(h, axis=1, keepdims=True) for h in hot]
    sums = dot(jnp.concatenate([h.astype(BF) for h in hot], axis=0), queries)
    masks, packed = [], []
    for e in range(2):
        sel = lo if e == 0 else ~lo
        safe = jnp.maximum(counts[e], 1.0)
        center = jnp.where(sel, sums[e * rows : (e + 1) * rows] / safe, 0.0).astype(BF)
        score = dot_nt(center, keys) * scale
        top = jnp.max(score, axis=1, keepdims=True)
        grown = jnp.exp(score - top)
        total = jnp.sum(grown, axis=1, keepdims=True)
        cprob = grown / total
        mask = top_mask(offs[0, e], expand[...], omod[...])
        mass = jnp.sum(jnp.where(mask, cprob, 0.0), axis=1, keepdims=True).astype(BF).astype(F32)
        kept = jnp.where(mask, 0.0, cprob).astype(BF)
        rest = jnp.where(sel, dot(kept, values), 0.0).astype(BF)
        wide = jnp.where(sel, mass, 0.0).astype(BF)
        packed.append(jnp.concatenate([rest, wide], axis=1))
        masks.append(jnp.where(mask, 1.0, 0.0).astype(BF))
        cen[0, e * rows : (e + 1) * rows, :] = center
        cst[0, e * rows : (e + 1) * rows, :] = jnp.where(
            lane == 0, top + jnp.log(total), jnp.where(lane == 1, safe, mass)
        )
    both = jnp.concatenate(packed, axis=0)
    rm[0] = both
    cluster_own = lax.broadcasted_iota(jnp.int32, (rows, own), 0)
    hot_own = [
        jnp.where(cluster_own == ids_own[0, e : e + 1, :], 1.0, 0.0).astype(BF) for e in range(2)
    ]
    token = dot_tn(jnp.concatenate(hot_own, axis=0), both)
    for t in range(own // tile):
        part = slice(t * tile, (t + 1) * tile)
        members, stats = [], []
        for e in range(2):
            sel = lo if e == 0 else ~lo
            query = jnp.where(sel, q_own[part, :], jnp.zeros((), BF))
            score = dot_nt(query, keys) * scale
            mask = dot_tn(hot_own[e][:, part], masks[e])
            score = jnp.where(mask > 0.5, score, NEG)
            top = jnp.max(score, axis=1, keepdims=True)
            grown = jnp.exp(score - top)
            total = jnp.sum(grown, axis=1, keepdims=True)
            weights = (grown * (1.0 / total)).astype(BF)
            prob[e, part, :] = weights
            members.append(dot(weights, values))
            stats.append(top + jnp.log(total))
        member = jnp.where(lo, members[0], members[1])
        mem[part, :] = member
        att[part, :] = (token[part, 128:] * member + token[part, :128]).astype(BF)
        table = jnp.where(lane == 0, stats[0], jnp.where(lane == 1, stats[1], 0.0))
        lse[0, :, part] = table.T[:8]


def ffn_body(info, x, cot, att_mine, att_other, wo_mine, wo_other, gain, bias, w_up, w_down,
             out, d_mid, d_attn, da_mine, da_other, normed_out, act_out, du_mine, du_send, vecs,
             mid_ref, n2_ref, acc, dacc):
    step = pl.program_id(0)
    steps = pl.num_programs(0)

    @pl.when(step == 0)
    def _():
        mid = x[...].astype(F32) + dot(att_mine[...], wo_mine[...]) + dot(att_other[...], wo_other[...])
        mid_ref[...] = mid
        xhat, _ = norm_parts(mid)
        normed = (xhat * gain[...] + bias[...]).astype(BF)
        n2_ref[...] = normed
        normed_out[...] = normed
        acc[...] = mid
        dacc[...] = jnp.zeros_like(dacc)

    upper = dot(n2_ref[...], w_up[...])
    c0 = math.sqrt(2.0 / math.pi)
    square = upper * upper
    tanh = jnp.tanh(c0 * (upper + 0.044715 * square * upper))
    cdf = 0.5 * (1.0 + tanh)
    active = (upper * cdf).astype(BF)
    act_out[...] = active
    acc[...] += dot(active, w_down[...])
    slope = cdf + 0.5 * upper * (1.0 - tanh * tanh) * (c0 * (1.0 + 3 * 0.044715 * square))
    d_upper = (dot_nt(cot[...], w_down[...]) * slope).astype(BF)
    half = d_upper.shape[1] // 2
    first = info[0] == 0
    du_mine[0] = jnp.where(first, d_upper[:, :half], d_upper[:, half:])
    du_send[0] = jnp.where(first, d_upper[:, half:], d_upper[:, :half])
    dacc[...] += dot_nt(d_upper, w_up[...])

    @pl.when(step == steps - 1)
    def _():
        out[...] = acc[...]
        xhat, rstd = norm_parts(mid_ref[...])
        d_normed = dacc[...]
        vecs[...] = jnp.concatenate(
            [
                jnp.sum(d_normed * xhat, axis=0, keepdims=True),
                jnp.sum(d_normed, axis=0, keepdims=True),
                jnp.zeros((6, d_normed.shape[1]), F32),
            ],
            axis=0,
        )
        grad = cot[...].astype(F32) + norm_back(d_normed, xhat, rstd, gain[...])
        d_mid[...] = grad
        low = grad.astype(BF)
        d_attn[...] = low
        da_mine[...] = dot_nt(low, wo_mine[...]).astype(BF)
        da_other[...] = dot_nt(low, wo_other[...]).astype(BF)


def join_body(info, mine, other, mem, joined, rows_out):
    core = info[0]
    block = mine.shape[0]
    lo = low_half()
    lane = lax.broadcasted_iota(jnp.int32, (1, 128), 1)
    for rel, ref in enumerate((mine, other)):
        rows = rows_at(core ^ rel, block)
        joined[rows, :] = ref[...]
        for p in range(mine.shape[1] // 128):
            part = slice(p * 128, (p + 1) * 128)
            product = ref[:, part].astype(F32) * mem[rows, part]
            first = jnp.sum(jnp.where(lo, product, 0.0), axis=1, keepdims=True)
            second = jnp.sum(jnp.where(lo, 0.0, product), axis=1, keepdims=True)
            table = jnp.where(lane == 0, first, jnp.where(lane == 1, second, 0.0))
            rows_out[p, :, rows] = table.T[:8]


def query_body(scale, tile, info, ids_own, datt, rm, prob, k_all, v_all, dq):
    keys, values = k_all[...], v_all[...]
    own = datt.shape[0]
    rows = rm.shape[1] // 2
    lo = low_half()
    cluster_own = lax.broadcasted_iota(jnp.int32, (rows, own), 0)
    hot_own = [
        jnp.where(cluster_own == ids_own[0, e : e + 1, :], 1.0, 0.0).astype(BF) for e in range(2)
    ]
    mass = dot_tn(jnp.concatenate(hot_own, axis=0), rm[0, :, 128:])
    d_member = (mass * datt[...].astype(F32)).astype(BF)
    for t in range(own // tile):
        part = slice(t * tile, (t + 1) * tile)
        found = []
        for e in range(2):
            sel = lo if e == 0 else ~lo
            grad = jnp.where(sel, d_member[part], jnp.zeros((), BF))
            d_prob = dot_nt(grad, values)
            weights = prob[e, part, :].astype(F32)
            moved = weights * d_prob
            d_score = (moved - weights * jnp.sum(moved, axis=1, keepdims=True)).astype(BF)
            found.append(dot(d_score, keys))
        dq[part, :] = jnp.where(lo, found[0], found[1]) * scale


def key_body(scale, slots, tile, info, ids, ids_own, offs, expand, omod, expand_own, omod_own,
             q_all, k_all, v_all, k_own, v_own, rm, cen, cst, dqm, *rest):
    datts, lses, dmasses = rest[:slots], rest[slots : 2 * slots], rest[2 * slots : 3 * slots]
    dq, dk, dv, datt, stat, d_mem, dcs = rest[3 * slots :]
    place = info[1]
    own = k_own.shape[0]
    keys, values, queries = k_all[...], v_all[...], q_all[...]
    full_len = keys.shape[0]
    rows = offs.shape[2]
    lo = low_half()
    for s in range(slots):
        at = lax.rem(place - s + slots, slots)
        datt[rows_at(at, own), :] = datts[s][...]
        stat[0, :, rows_at(at, own)] = lses[s][0]
        stat[1, :, rows_at(at, own)] = dmasses[s][0]
    cluster = lax.broadcasted_iota(jnp.int32, (rows, full_len), 0)
    hits = [cluster == ids[0, e : e + 1, :] for e in range(2)]
    hot = [jnp.where(h, 1.0, 0.0).astype(BF) for h in hits]
    hot_both = jnp.concatenate(hot, axis=0)
    d_rest_both = dot(hot_both, datt[...])
    mass_token = dot_tn(hot_both, rm[0, :, 128:])
    d_mem[...] = (mass_token * datt[...].astype(F32)).astype(BF)
    d_sums, rests, keeps, mass_rows = [], [], [], []
    for e in range(2):
        sel = lo if e == 0 else ~lo
        part = slice(e * rows, (e + 1) * rows)
        log_total, safe, mass = cst[0, part, 0:1], cst[0, part, 1:2], cst[0, part, 2:3]
        mass_rows.append(jnp.sum(jnp.where(hits[e], mass, 0.0), axis=0, keepdims=True))
        d_rest = jnp.where(sel, d_rest_both[part], 0.0).astype(BF)
        d_mass = jnp.sum(jnp.where(hits[e], stat[1, e : e + 1, :], 0.0), axis=1, keepdims=True)
        center = cen[0, part, :]
        cprob = jnp.exp(dot_nt(center, keys) * scale - log_total)
        mask = top_mask(offs[0, e], expand[...], omod[...])
        d_prob = jnp.where(mask, d_mass, dot_nt(d_rest, values))
        moved = cprob * d_prob
        d_score = (moved - cprob * jnp.sum(moved, axis=1, keepdims=True)).astype(BF)
        dcs[0, part, :] = d_score
        dcs[1, part, :] = jnp.where(mask, 0.0, cprob).astype(BF)
        d_center = jnp.where(sel, dot(d_score, keys) * (scale / safe), 0.0)
        d_sums.append(d_center.astype(BF))
        rests.append(d_rest)
    cluster_own = lax.broadcasted_iota(jnp.int32, (rows, own), 0)
    hot_own = jnp.concatenate(
        [
            jnp.where(cluster_own == ids_own[0, e : e + 1, :], 1.0, 0.0).astype(BF)
            for e in range(2)
        ],
        axis=0,
    )
    dq[...] = (dqm[...] + dot_tn(hot_own, jnp.concatenate(d_sums, axis=0))).astype(BF)
    columns = rows_at(place, own)
    d_key = dot_tn(dcs[0, :, columns], cen[0])
    d_value = dot_tn(dcs[1, :, columns], jnp.concatenate(rests, axis=0))
    masks_own = [
        jnp.where(top_mask(offs[0, e], expand_own[...], omod_own[...]), 1.0, 0.0).astype(BF)
        for e in range(2)
    ]
    key_sides = [jnp.where(lo if e == 0 else ~lo, k_own[...], jnp.zeros((), BF)) for e in range(2)]
    value_sides = [
        jnp.where(lo if e == 0 else ~lo, v_own[...], jnp.zeros((), BF)) for e in range(2)
    ]
    dks, dvs = [0.0, 0.0], [0.0, 0.0]
    for t in range(full_len // tile):
        part = slice(t * tile, (t + 1) * tile)
        grad = d_mem[part, :]
        query = queries[part]
        for e in range(2):
            score = dot_nt(key_sides[e], query) * scale
            mask = dot_tn(masks_own[e], hot[e][:, part])
            weights = jnp.exp(jnp.where(mask > 0.5, score - stat[0, e : e + 1, part], NEG))
            d_prob = dot_nt(value_sides[e], grad)
            delta = mass_rows[e][:, part] * stat[1, e : e + 1, part]
            d_score = (weights * (d_prob - delta)).astype(BF)
            dvs[e] += dot(weights.astype(BF), grad)
            dks[e] += dot(d_score, query)
    dk[...] = ((jnp.where(lo, dks[0], dks[1]) + d_key) * scale).astype(BF)
    dv[...] = (jnp.where(lo, dvs[0], dvs[1]) + d_value).astype(BF)


def emit_chunks(info, flat, outs, places, q_count, per):
    core, place, mine = info[0], info[1], info[2]
    for r in range(q_count):
        rows = rows_at(mine ^ r, per)
        for rel in range(2):
            for s in range(places):
                at = lax.rem(place + s, places)
                outs[2 * r + rel][s] = flat[at, core ^ rel, rows, :]


def store_rows(flat, value, row, chunk):
    for owner in range(value.shape[0] // chunk):
        flat[owner // 2, owner % 2, row : row + chunk, :] = value[
            owner * chunk : (owner + 1) * chunk
        ].astype(BF)


def store_vecs(flat, vecs, row):
    half = vecs.shape[1] // 2
    lines = jnp.concatenate(
        [vecs[0:1, :half], vecs[0:1, half:], vecs[1:2, :half], vecs[1:2, half:]]
        + [jnp.zeros((12, half), F32)],
        axis=0,
    ).astype(BF)
    for z in range(flat.shape[0]):
        for c in range(2):
            flat[z, c, row : row + 16, :] = lines


def ffn_grad_body(places, q_count, per, info, n_mine, n_other, du_mine, du_other, act_mine, act_other,
                  cot_mine, cot_other, att_mine, att_other, da_mine, da_other, vecs, *rest):
    outs, (flat,) = rest[:-1], rest[-1:]
    core = info[0]
    width = n_mine.shape[1]
    chunk = width // (2 * places)
    step_count = du_mine.shape[0]
    hidden = act_mine.shape[1]
    down_chunk = hidden // (2 * places)
    block = n_mine.shape[0]
    n_t = [n_mine[...].T, n_other[...].T]
    for f in range(step_count):
        up = dot(n_t[0], du_mine[f]) + dot(n_t[1], du_other[f])
        store_rows(flat, up, f * chunk, chunk)
    base = step_count * chunk
    span = hidden // step_count
    for f in range(step_count):
        part = slice(f * span, (f + 1) * span)
        down = dot_tn(act_mine[:, part], cot_mine[...]) + dot_tn(act_other[:, part], cot_other[...])
        for i in range(span // down_chunk):
            owner = f * (span // down_chunk) + i
            flat[owner // 2, owner % 2, base : base + down_chunk, :] = down[
                i * down_chunk : (i + 1) * down_chunk
            ].astype(BF)
    base += down_chunk
    mine_rows, other_rows = rows_at(core, block), rows_at(1 - core, block)
    halves = []
    for ref in (att_mine, att_other):
        halves.append(
            dot_tn(ref[mine_rows, :], da_mine[...]) + dot_tn(ref[other_rows, :], da_other[...])
        )
    first = core == 0
    store_rows(
        flat,
        jnp.concatenate(
            [jnp.where(first, halves[0], halves[1]), jnp.where(first, halves[1], halves[0])], axis=0
        ),
        base,
        chunk,
    )
    base += chunk
    store_vecs(flat, vecs[...], base)
    emit_chunks(info, flat, outs, places, q_count, per)


def qkv_grad_body(places, q_count, per, info, normed, dq, dk, dv, wq, wk, wv, xa, xb, *rest):
    dn_mine, dn_send = rest[0], rest[1]
    outs, flat = rest[2:-1], rest[-1]
    core = info[0]
    block, width = xa.shape
    chunk = width // (2 * places)
    n_t = normed[...].T
    for i, ref in enumerate((dq, dk, dv)):
        store_rows(flat, dot(n_t, ref[...]), i * chunk, chunk)
    gains, biases = 0.0, 0.0
    for rel, (ref, out) in enumerate(((xa, dn_mine), (xb, dn_send))):
        rows = rows_at(core ^ rel, block)
        d_normed = (
            dot_nt(dq[rows, :], wq[...]) + dot_nt(dk[rows, :], wk[...]) + dot_nt(dv[rows, :], wv[...])
        )
        out[...] = d_normed
        xhat, _ = norm_parts(ref[...].astype(F32))
        gains += jnp.sum(d_normed * xhat, axis=0, keepdims=True)
        biases += jnp.sum(d_normed, axis=0, keepdims=True)
    store_vecs(flat, jnp.concatenate([gains, biases], axis=0), 3 * chunk)
    emit_chunks(info, flat, outs, places, q_count, per)


def input_body(info, x, gain, dn_mine, dn_other, d_mid, out):
    xhat, rstd = norm_parts(x[...].astype(F32))
    out[...] = d_mid[...] + norm_back(dn_mine[...] + dn_other[...], xhat, rstd, gain[...])


def gather_flat(info, mine, other, flat, per):
    own = info[2]
    for r in range(len(mine)):
        rows = rows_at(own ^ r, per)
        flat[0, rows, :] = mine[r][...]
        flat[1, rows, :] = other[r][...]


def ffn_out_body(q_count, per, info, *rest):
    mine, other = rest[:q_count], rest[q_count : 2 * q_count]
    up, down, out, vec, flat = rest[2 * q_count :]
    gather_flat(info, mine, other, flat, per)
    core = info[0]
    half = flat.shape[2]
    chunk = up.shape[0]
    steps = up.shape[1] // (2 * half)
    for c in range(2):
        src = core ^ c
        for f in range(steps):
            at = (2 * f + c) * half
            up[:, at : at + half] = flat[src, f * chunk : (f + 1) * chunk, :].astype(F32)
        base = steps * chunk
        down[:, c * half : (c + 1) * half] = flat[src, base : base + down.shape[0], :].astype(F32)
        base += down.shape[0]
        out[:, c * half : (c + 1) * half] = flat[src, base : base + chunk, :].astype(F32)
        base += chunk
    vec[...] = flat[0, base : base + 16, :].astype(F32) + flat[1, base : base + 16, :].astype(F32)


def qkv_out_body(q_count, per, info, *rest):
    mine, other = rest[:q_count], rest[q_count : 2 * q_count]
    outs, vec, flat = rest[2 * q_count : 2 * q_count + 3], rest[-2], rest[-1]
    gather_flat(info, mine, other, flat, per)
    core = info[0]
    half = flat.shape[2]
    chunk = outs[0].shape[0]
    for c in range(2):
        src = core ^ c
        for i, out in enumerate(outs):
            out[:, c * half : (c + 1) * half] = flat[src, i * chunk : (i + 1) * chunk, :].astype(F32)
    base = 3 * chunk
    vec[...] = flat[0, base : base + 16, :].astype(F32) + flat[1, base : base + 16, :].astype(F32)


def per_device(tokens, gain_one, bias_one, w_query, w_key, w_value, w_out, gain_two, bias_two,
               w_up, w_down, cotangent, cluster_ids, top_keys):
    _, block, width = tokens.shape
    heads = cluster_ids.shape[2]
    clusters, chosen = top_keys.shape[2], top_keys.shape[3]
    ctx, q_count = lax.axis_size("ctx"), lax.axis_size("seq")
    places = ctx // 2
    index, mine = lax.axis_index("ctx"), lax.axis_index("seq")
    core, place = index % 2, index // 2
    full_len = block * ctx
    own = 2 * block
    half = width // 2
    hidden = w_up.shape[1]
    pairs = half // 128
    stride = full_len // chosen
    rows = -(-clusters // 128) * 128
    scale = 1.0 / math.sqrt(width // heads)
    info = jnp.stack([core, place, mine]).astype(jnp.int32)

    swap_to = [(i, i ^ 1) for i in range(ctx)]

    def swap(a):
        return lax.ppermute(a, "ctx", swap_to)

    def along(a, s):
        to = [(2 * z + c, 2 * ((z + s) % places) + c) for z in range(places) for c in range(2)]
        return lax.ppermute(a, "ctx", to)

    def across(a, r):
        return lax.ppermute(a, "seq", [(i, i ^ r) for i in range(q_count)])

    x, cot = tokens[0], cotangent[0]
    gain1, bias1 = gain_one[None], bias_one[None]
    gain2, bias2 = gain_two[None], bias_two[None]

    x_other = swap(x)
    came = [along(x, s) for s in range(1, places)]
    came_other = [swap(a) for a in came]
    cot_other = swap(cot)
    ids_all = lax.all_gather(cluster_ids[0].T, "ctx", axis=1, tiled=True)
    ids = lax.dynamic_slice_in_dim(ids_all, core * (heads // 2), heads // 2, 0)
    ids = ids.reshape(pairs, 2, full_len)
    offs = top_keys[0] - jnp.arange(chosen, dtype=jnp.int32) * stride
    offs = lax.dynamic_slice_in_dim(offs, core * (heads // 2), heads // 2, 0).astype(BF)
    offs = jnp.pad(offs, ((0, 0), (0, rows - clusters), (0, 0))).reshape(pairs, 2, rows, chosen)
    spots = np.arange(full_len)
    expand = jnp.asarray(spots[None] // stride == np.arange(chosen)[:, None], BF)
    omod = jnp.asarray(spots[None] % stride, F32)

    def slot(s):
        return info.at[1].set(lax.rem(place - s + places, places))

    query, key, value, normed = qkv_call(
        info, x, x_other, gain1, bias1, w_query, w_key, w_value, full_len, None
    )
    for s in range(1, places):
        query, key, value = qkv_call(
            slot(s), came[s - 1], came_other[s - 1], gain1, bias1, w_query, w_key, w_value,
            full_len, (query, key, value),
        )

    pair_all = pl.BlockSpec((full_len, 128), lambda p, s: (0, p))
    pair_own = pl.BlockSpec((own, 128), lambda p, s: (s[1], p))
    pair_loc = pl.BlockSpec((own, 128), lambda p, s: (0, p))
    ids_spec = pl.BlockSpec((1, 2, full_len), lambda p, s: (p, 0, 0))
    ids_own_spec = pl.BlockSpec((1, 2, own), lambda p, s: (p, 0, s[1]))
    offs_spec = pl.BlockSpec((1, 2, rows, chosen), lambda p, s: (p, 0, 0, 0))
    expand_own_spec = pl.BlockSpec((chosen, own), lambda p, s: (0, s[1]))
    omod_own_spec = pl.BlockSpec((1, own), lambda p, s: (0, s[1]))
    prob_spec = pl.BlockSpec((2, own, full_len), lambda p, s: (p, 0, 0))
    stat_spec = pl.BlockSpec((1, 8, own), lambda p, s: (p, 0, 0))
    rm_spec = pl.BlockSpec((1, 2 * rows, 256), lambda p, s: (p, 0, 0))
    cen_spec = pl.BlockSpec((1, 2 * rows, 128), lambda p, s: (p, 0, 0))
    sds = jax.ShapeDtypeStruct
    tile = min(256, own)

    att, mem, prob, lse, rm, cen, cst = call(
        functools.partial(fwd_body, scale, tile),
        (pairs,),
        [ids_spec, ids_own_spec, offs_spec, full((chosen, full_len)), full((1, full_len)),
         pair_all, pair_all, pair_all, pair_own],
        [pair_loc, pair_loc, prob_spec, stat_spec, rm_spec, cen_spec, cen_spec],
        [sds((own, half), BF), sds((own, half), F32), sds((2 * pairs, own, full_len), BF),
         sds((pairs, 8, own), F32), sds((pairs, 2 * rows, 256), BF),
         sds((pairs, 2 * rows, 128), BF), sds((pairs, 2 * rows, 128), F32)],
        flops=heads * own * full_len * 64 * 3,
        moved=own * full_len * heads,
    )(info, ids, ids, offs, expand, omod, query, key, value, query)

    att_other = swap(att)
    lse_all = [lse] + [along(lse, s) for s in range(1, places)]

    steps = hidden // width
    whole = full((block, width))
    att_spec = pl.BlockSpec((block, half), lambda f, s: (s[0], 0))
    out, d_mid, d_attn, da_mine, da_send, normed_two, act, du_mine, du_send, vecs_two = call(
        ffn_body,
        (steps,),
        [whole, whole, att_spec, att_spec,
         pl.BlockSpec((half, width), lambda f, s: (s[0], 0)),
         pl.BlockSpec((half, width), lambda f, s: (1 - s[0], 0)),
         full((1, width)), full((1, width)),
         pl.BlockSpec((width, width), lambda f, s: (0, f)),
         pl.BlockSpec((width, width), lambda f, s: (f, 0))],
        [whole, whole, whole, full((block, half)), full((block, half)), whole,
         pl.BlockSpec((block, width), lambda f, s: (0, f)),
         pl.BlockSpec((1, block, half), lambda f, s: (f, 0, 0)),
         pl.BlockSpec((1, block, half), lambda f, s: (f, 0, 0)),
         full((8, width))],
        [sds((block, width), F32), sds((block, width), F32), sds((block, width), BF),
         sds((block, half), BF), sds((block, half), BF), sds((block, width), BF),
         sds((block, hidden), BF), sds((steps, block, half), BF), sds((steps, block, half), BF),
         sds((8, width), F32)],
        scratch=[pltpu.VMEM((block, width), F32), pltpu.VMEM((block, width), BF),
                 pltpu.VMEM((block, width), F32), pltpu.VMEM((block, width), F32)],
        flops=8 * block * width * hidden,
        moved=4 * width * hidden,
    )(info, x, cot, att, att_other, w_out, w_out, gain2, bias2, w_up, w_down)

    datt, dmass = call(
        join_body,
        (1,),
        [full((block, half)), full((block, half)), full((own, half))],
        [full((own, half)), full((pairs, 8, own))],
        [sds((own, half), BF), sds((pairs, 8, own), F32)],
        moved=own * half * 8,
    )(info, da_mine, swap(da_send), mem)
    datt_all = [datt] + [along(datt, s) for s in range(1, places)]
    dmass_all = [dmass] + [along(dmass, s) for s in range(1, places)]

    dqm = call(
        functools.partial(query_body, scale, tile),
        (pairs,),
        [ids_own_spec, pair_loc, rm_spec, prob_spec, pair_all, pair_all],
        [pair_loc],
        [sds((own, half), F32)],
        flops=heads * own * full_len * 64 * 2,
        moved=own * full_len * heads,
    )(info, ids, datt, rm, prob, key, value)[0]

    chunk, down_chunk = width // ctx, hidden // ctx
    def padded(n):
        return -(-n // (16 * q_count)) * 16 * q_count

    ffn_rows = padded(steps * chunk + down_chunk + chunk + 16)
    per = ffn_rows // q_count
    cot_spec = pl.BlockSpec((block, half), lambda i, s: (0, s[0]))
    pieces = call(
        functools.partial(ffn_grad_body, places, q_count, per),
        (1,),
        [whole, whole, full((steps, block, half)), full((steps, block, half)),
         full((block, hidden)), full((block, hidden)), cot_spec, cot_spec,
         full((own, half)), full((own, half)), cot_spec, cot_spec, full((8, width))],
        [full((places, per, half))] * (2 * q_count),
        [sds((places, per, half), BF)] * (2 * q_count),
        scratch=[pltpu.VMEM((places, 2, ffn_rows, half), BF)],
        flops=4 * own * hidden * half + 2 * own * width * half,
        moved=2 * places * ffn_rows * half * 2,
    )(info, normed_two, swap(normed_two), du_mine, swap(du_send), act, swap(act), cot, cot_other,
      att, att_other, d_attn, swap(d_attn), vecs_two)

    def add(a, b):
        return (a.astype(F32) + b.astype(F32)).astype(BF)

    def reduce_seq(parts, bits):
        parts = dict(enumerate(parts))
        for bit in bits:
            sent = {r: across(parts[r], bit) for r in parts if r & bit}
            parts = {r: add(parts[r], sent[r | bit]) for r in parts if not r & bit}
        return parts[0]

    def reduce_along(whole_part):
        total = whole_part[0].astype(F32)
        for s in range(1, places):
            total = total + along(whole_part[s], s).astype(F32)
        return total.astype(BF)

    def spread_seq(part):
        return [part] + [across(part, r) for r in range(1, q_count)]

    bits = [1 << i for i in range((q_count - 1).bit_length())]

    def reduce_all(pieces):
        own_part = reduce_along(reduce_seq(pieces[0::2], bits))
        send_part = reduce_along(reduce_seq(pieces[1::2], bits[::-1]))
        return spread_seq(own_part) + spread_seq(swap(send_part))

    ffn_parts = reduce_all(pieces)

    dq, dk, dv = call(
        functools.partial(key_body, scale, places, min(512, full_len)),
        (pairs,),
        [ids_spec, ids_own_spec, offs_spec, full((chosen, full_len)), full((1, full_len)),
         expand_own_spec, omod_own_spec, pair_all, pair_all, pair_all, pair_own, pair_own,
         rm_spec, cen_spec, cen_spec, pair_loc] + [pair_loc] * places + [stat_spec] * (2 * places),
        [pair_loc] * 3,
        [sds((own, half), BF)] * 3,
        scratch=[pltpu.VMEM((full_len, 128), BF), pltpu.VMEM((2, 8, full_len), F32),
                 pltpu.VMEM((full_len, 128), BF), pltpu.VMEM((2, 2 * rows, full_len), BF)],
        flops=heads * own * full_len * 64 * 5,
        moved=own * full_len * 4,
    )(info, ids, ids, offs, expand, omod, expand, omod, query, key, value, key, value, rm, cen, cst,
      dqm, *datt_all, *lse_all, *dmass_all)

    qkv_rows = padded(3 * chunk + 16)
    per_one = qkv_rows // q_count
    weight = pl.BlockSpec((width, half), lambda i, s: (0, s[0]))
    dn_mine, dn_send, *pieces = call(
        functools.partial(qkv_grad_body, places, q_count, per_one),
        (1,),
        [full((own, width))] + [full((own, half))] * 3 + [weight] * 3 + [whole] * 2,
        [whole] * 2 + [full((places, per_one, half))] * (2 * q_count),
        [sds((block, width), F32)] * 2 + [sds((places, per_one, half), BF)] * (2 * q_count),
        scratch=[pltpu.VMEM((places, 2, qkv_rows, half), BF)],
        flops=12 * own * width * half,
        moved=2 * places * qkv_rows * half * 2,
    )(info, normed, dq, dk, dv, w_query, w_key, w_value, x, x_other)
    qkv_parts = reduce_all(pieces)

    input_grad = call(
        input_body,
        (1,),
        [whole, full((1, width)), whole, whole, whole],
        [whole],
        [sds((block, width), F32)],
        moved=block * width * 18,
    )(info, x, gain1, dn_mine, swap(dn_send), d_mid)[0]

    grad_up, grad_down, grad_out, vec_two = call(
        functools.partial(ffn_out_body, q_count, per),
        (1,),
        [full((per, half))] * (2 * q_count),
        [full((chunk, hidden)), full((down_chunk, width)), full((chunk, width)), full((16, half))],
        [sds((chunk, hidden), F32), sds((down_chunk, width), F32), sds((chunk, width), F32),
         sds((16, half), F32)],
        scratch=[pltpu.VMEM((2, ffn_rows, half), BF)],
        moved=ffn_rows * width * 6,
    )(info, *ffn_parts)
    grad_query, grad_key, grad_value, vec_one = call(
        functools.partial(qkv_out_body, q_count, per_one),
        (1,),
        [full((per_one, half))] * (2 * q_count),
        [full((chunk, width))] * 3 + [full((16, half))],
        [sds((chunk, width), F32)] * 3 + [sds((16, half), F32)],
        scratch=[pltpu.VMEM((2, qkv_rows, half), BF)],
        moved=qkv_rows * width * 6,
    )(info, *qkv_parts)

    def vectors(vec):
        both = vec[:4].reshape(2, width)
        cut = lax.dynamic_slice_in_dim(both, index * chunk, chunk, 1)
        return cut[0], cut[1]

    grad_gain_one, grad_bias_one = vectors(vec_one)
    grad_gain_two, grad_bias_two = vectors(vec_two)
    return (out[None], input_grad[None], grad_gain_one, grad_bias_one, grad_query, grad_key,
            grad_value, grad_out, grad_gain_two, grad_bias_two, grad_up, grad_down)


def solution(mesh):
    split = P("seq", "ctx", None)
    in_specs = (split,) + (P(),) * 10 + (split, split, P("seq", None, None, None))
    vec, mat = P("ctx"), P("ctx", None)
    out_specs = (split, split, vec, vec, mat, mat, mat, mat, vec, vec, mat, mat)
    return jax.shard_map(
        per_device, mesh=mesh, in_specs=in_specs, out_specs=out_specs, check_vma=False
    )
```

time: 1050 us -> 371 us (0.35)
  waiting for transfers between devices: 435 us -> 109 us
  local copies, waits for them, and re-layouts: 205 us -> 16.7 us
  blocking collectives: 219 us -> 39.6 us
  Pallas kernels: 0 us -> 131 us
  matrix products: 123 us -> 0 us
  starting transfers between devices: 0.92 us -> 63.8 us
  other arithmetic: 44.6 us -> 2.49 us
  between operations: 16.9 us -> 1.5 us
    reduce_scatter x8 -> x0, waiting for transfers between devices: 371 us -> none  [the longest x1 101 us: per_device(): lax.psum_scatter(down_weight_gradient, 'ctx', scatter_dimension=0, tiled=...]
    unnamed x3 -> x0, blocking collectives: 162 us -> none
    pallas_call x0 -> x14, Pallas kernels: none -> 131 us  [the longest x1 31.9 us: per_device(): call(functools.partial(key_body, scale, places, min(512, full_len)), (pai...]
    dot_general x35 -> x0, matrix products: 119 us -> none  [the longest x6 24.9 us: weight_grad(): jnp.einsum('sli,slj->ij', left_side, gradient_value, preferred_element_ty...]
    ppermute x0 -> x62, waiting for transfers between devices: none -> 109 us  [the longest x24 55.9 us: along(): return lax.ppermute(a, 'ctx', to)]
    gather x5 -> x0, local copies, waits for them, and re-layouts: 84.6 us -> none  [the longest x3 48.4 us: per_device(): jnp.take_along_axis(cprob, my_keys, axis=3)]
    unnamed x191 -> x99, local copies, waits for them, and re-layouts: 94.7 us -> 13.9 us
    ppermute x0 -> x62, starting transfers between devices: none -> 63.8 us  [the longest x24 34.5 us: along(): return lax.ppermute(a, 'ctx', to)]
  transfers between devices with their start and end apart: 12 -> 62, of which waited for: 9 -> 19; matrix products, arithmetic and copies ran while one was open for 27% -> 1% of each run, Pallas kernels for 0% -> 22%
where the time goes in v1:
time: 371 us; the launch traced here: 364 us
  Pallas kernels  131 us (35%)
  waiting for transfers between devices  109 us (29%)
  starting transfers between devices  63.8 us (17%)
  blocking collectives  39.6 us (11%)
  local copies, waits for them, and re-layouts  16.7 us (5%)
    ppermute x24, waiting for transfers between devices, along(): return lax.ppermute(a, 'ctx', to)  55.9 us
    ppermute x24, waiting for transfers between devices, across(): return lax.ppermute(a, 'seq', [(i, i ^ r) for i in range(q_count)])  50.3 us
    all_gather x1, blocking collectives, per_device(): ids_all = lax.all_gather(cluster_ids[0].T, 'ctx', axis=1, tiled=True)  39.6 us
    ppermute x24, starting transfers between devices, along(): return lax.ppermute(a, 'ctx', to)  34.5 us
    pallas_call x1, Pallas kernels, per_device(): call(functools.partial(key_body, scale, places, min(512, full_len)), (pai...  31.9 us
    pallas_call x1, Pallas kernels, per_device(): call(functools.partial(fwd_body, scale, tile), (pairs,), [ids_spec, ids_o...  29.5 us
    ppermute x24, starting transfers between devices, across(): return lax.ppermute(a, 'seq', [(i, i ^ r) for i in range(q_count)])  26.6 us
    pallas_call x4, Pallas kernels, qkv_call(): call(functools.partial(qkv_body, first), (1,), in_specs, out_specs, out_s...  17.3 us
  transfers between devices with their start and end apart: 62, of which 19 were waited for; matrix products, arithmetic and copies ran while one was open for 1% of the time, Pallas kernels for 22%

profile of v1, /device:TPU:0, one launch (start us, length us, event | category | flops | bytes accessed | tf_op | source)
XLA Modules:
  0.0 363.7 jit_solution(6741326265851307999)
XLA Ops:
  0.7 3.1 collective-permute-start.4
  3.7 2.1 collective-permute-start
  5.8 0.9 collective-permute-start.2
  7.5 39.6 %all_gather.3 = s32[12,2048]{1,0:T(8,128)S(1)} all-gather(s32[12,256]{1,0:T(8,128)S(1)} %bitcast.83), channel_id=1, replica_groups=mesh['seq'=4,'ctx'=8] {'ctx'}, dimensions={1}, use_global_device_ids=true | all-gather | bytes 110592 | tf_op jit(solution)/shard_map/all_gather | solution.py:551
  48.2 1.0 fusion.12
  50.8 4.4 %shard_map.247 = (bf16[2048,384]{1,0:T(8,128)(2,1)}, bf16[2048,384]{1,0:T(8,128)(2,1)}, bf16[2048,384]{1,0:T(8,128)(2,1)}, bf16[512,768]{1,0:T(8,128)(2,1)S(1)}) custom-call(s32[3]{0:T(128)S(1)} %pad_add_fusion.info, bf16[256,768]{1,0:T(8,128)(2,1)S(1)} %bitcast.74, bf16[256,768]{1,0:T(8,128)(2,1)S(1)} %collective-permute-done.6.xb, ...), custom_call_target="tpu_custom_call" | custom-call | flops 905969664 | bytes 1769472 | tf_op jit(solution)/shard_map/pallas_call | solution.py:111
  55.3 4.3 %shard_map.248 = (bf16[2048,384]{1,0:T(8,128)(2,1)}, bf16[2048,384]{1,0:T(8,128)(2,1)}, bf16[2048,384]{1,0:T(8,128)(2,1)}) custom-call(s32[3]{0:T(128)S(1)} %constant_dynamic-update-slice_fusion.info, bf16[256,768]{1,0:T(8,128)(2,1)S(1)} %collective-permute-done.4.xa, ...), custom_call_target="tpu_custom_call", output_to_operand_aliasing={{0}: (8, {}), {1}: (9, {}), {2}: (10, {})} | custom-call | flops 905969664 | bytes 1769472 | tf_op jit(solution)/shard_map/pallas_call | solution.py:111
  59.6 4.3 %shard_map.249 = (bf16[2048,384]{1,0:T(8,128)(2,1)}, bf16[2048,384]{1,0:T(8,128)(2,1)}, bf16[2048,384]{1,0:T(8,128)(2,1)}) custom-call(s32[3]{0:T(128)S(1)} %constant_dynamic-update-slice_fusion.1.info, bf16[256,768]{1,0:T(8,128)(2,1)S(1)} %collective-permute-done.2.xa, ...), custom_call_target="tpu_custom_call", output_to_operand_aliasing={{0}: (8, {}), {1}: (9, {}), {2}: (10, {})} | custom-call | flops 905969664 | bytes 1769472 | tf_op jit(solution)/shard_map/pallas_call | solution.py:111
  63.9 4.3 %shard_map.250 = (bf16[2048,384]{1,0:T(8,128)(2,1)}, bf16[2048,384]{1,0:T(8,128)(2,1)}, bf16[2048,384]{1,0:T(8,128)(2,1)}) custom-call(s32[3]{0:T(128)S(1)} %constant_dynamic-update-slice_fusion.2.info, bf16[256,768]{1,0:T(8,128)(2,1)S(1)} %collective-permute-done.xa, ...), custom_call_target="tpu_custom_call", output_to_operand_aliasing={{0}: (8, {}), {1}: (9, {}), {2}: (10, {})} | custom-call | flops 905969664 | bytes 1769472 | tf_op jit(solution)/shard_map/pallas_call | solution.py:111
  68.2 29.5 %shard_map.251 = (bf16[512,384]{1,0:T(8,128)(2,1)S(1)}, f32[512,384]{1,0:T(8,128)}, bf16[6,512,2048]{2,1,0:T(8,128)(2,1)}, f32[3,8,512]{2,1,0:T(8,128)S(1)}, bf1...) custom-call(s32[3]{0:T(128)S(1)} %pad_add_fusion.info, ...), custom_call_target="tpu_custom_call" | custom-call | flops 2415919104 | bytes 12582912 | tf_op jit(solution)/shard_map/pallas_call | solution.py:588
  98.0 1.5 collective-permute-done.7.att_other
  100.3 13.5 %shard_map.252 = (f32[256,768]{1,0:T(8,128)}, f32[256,768]{1,0:T(8,128)}, bf16[256,768]{1,0:T(8,128)(2,1)S(1)}, bf16[256,384]{1,0:T(8,128)(2,1)S(1)}, bf16[256,3...) custom-call(s32[3]{0:T(128)S(1)} %pad_add_fusion.info, ...), custom_call_target="tpu_custom_call" | custom-call | flops 4831838208 | bytes 9437184 | tf_op jit(solution)/shard_map/pallas_call | solution.py:607
  114.0 1.3 collective-permute-done.8.other
  115.3 1.2 shard_map.253
  116.9 2.4 collective-permute-start.10
  119.3 1.0 collective-permute-start.11
  120.4 1.0 collective-permute-start.12
  121.4 1.0 collective-permute-start.13
  122.4 25.8 %collective-permute-done.12.rest_5_ = f32[3,8,512]{2,1,0:T(8,128)S(1)} collective-permute-done((f32[3,8,512]{2,1,0:T(8,128)S(1)}, f32[3,8,512]{2,1,0:T(8,128)S(1)}, u32[]{:S(2)}, u32[]{:S(2)}) %collective-permute-start.12) | collective-permute-done | bytes 49184 | tf_op jit(solution)/shard_map/ppermute | solution.py:538
  148.2 9.6 %collective-permute-done.13.rest_6_ = f32[3,8,512]{2,1,0:T(8,128)S(1)} collective-permute-done((f32[3,8,512]{2,1,0:T(8,128)S(1)}, f32[3,8,512]{2,1,0:T(8,128)S(1)}, u32[]{:S(2)}, u32[]{:S(2)}) %collective-permute-start.13) | collective-permute-done | bytes 49184 | tf_op jit(solution)/shard_map/ppermute | solution.py:538
  157.8 3.8 %collective-permute-start.16 = (f32[3,8,512]{2,1,0:T(8,128)S(1)}, f32[3,8,512]{2,1,0:T(8,128)S(1)}, u32[]{:S(2)}, u32[]{:S(2)}) collective-permute-start(f32[3,8,512]{2,1,0:T(8,128)S(1)} %get-tuple-element.133.rest_8_), channel_id=1, source_target_pairs={{0,4},{1,5},{2,6},{3,7},{4,0},{5,1},{6,2},{7,3},{8,12},{9,13},{10,... | collective-permute-start | bytes 147464 | tf_op jit(solution)/shard_map/ppermute | solution.py:538
  161.6 2.1 collective-permute-done.15.rest_9_
  163.7 14.0 %shard_map.254.dqm = f32[512,384]{1,0:T(8,128)S(1)} custom-call(s32[3]{0:T(128)S(1)} %pad_add_fusion.info, s32[3,2,2048]{2,1,0:T(2,128)S(1)} %reshape.111.ids.ids_own, bf16[512,384]{1,0:T(8,128)(2,1)S(1)} %get-tuple-element.130.datt.rest_0_, bf16[3,256,256]{2,1,0:T(8,128)(2,1)S(1)} %get-tuple-element.124.rm, bf16[6,512,2048]{2,1,0:T(8,128)(2,1)} %get-tuple-element.131.prob, ...), custom_call_target="tpu_custom_call" | custom-call | flops 1610612736 | bytes 12582912 | tf_op jit(solution)/shard_map/pallas_call | solution.py:642
  177.7 0.9 copy-done.3
  179.7 31.9 %shard_map.255 = (bf16[512,384]{1,0:T(8,128)(2,1)S(1)}, bf16[512,384]{1,0:T(8,128)(2,1)S(1)}, bf16[512,384]{1,0:T(8,128)(2,1)}) custom-call(s32[3]{0:T(128)S(1)} %pad_add_fusion.info, s32[3,2,2048]{2,1,0:T(2,128)S(1)} %reshape.111.ids.ids_own, s32[3,2,2048]{2,1,0:T(2,128)S(1)} %reshape.111.ids.ids_own, bf16[3,2,128,32]{3,2,1,0:T(8,128)(2,1)S(1)} %bitcast.78, ...), custom_call_target="tpu_custom_call" | custom-call | flops 4026531840 | bytes 4194304 | tf_op jit(solution)/shard_map/pallas_call | solution.py:701
  213.1 6.9 %shard_map.256 = (f32[256,768]{1,0:T(8,128)}, f32[256,768]{1,0:T(8,128)}, bf16[4,80,384]{2,1,0:T(8,128)(2,1)S(1)}, bf16[4,80,384]{2,1,0:T(8,128)(2,1)S(1)}, bf16...) custom-call(s32[3]{0:T(128)S(1)} %pad_add_fusion.info, ...), custom_call_target="tpu_custom_call" | custom-call | flops 1811939328 | bytes 1966080 | tf_op jit(solution)/shard_map/pallas_call | solution.py:719
  220.0 1.5 collective-permute-start.20
  222.2 1.5 collective-permute-start.29
  223.7 5.0 %collective-permute-done.20 = bf16[4,80,384]{2,1,0:T(8,128)(2,1)S(1)} collective-permute-done((bf16[4,80,384]{2,1,0:T(8,128)(2,1)S(1)}, bf16[4,80,384]{2,1,0:T(8,128)(2,1)S(1)}, u32[]{:S(2)}, u32[]{:S(2)}) %collective-permute-start.20) | collective-permute-done | bytes 245792 | tf_op jit(solution)/shard_map/ppermute | solution.py:541
  228.8 1.6 collective-permute-start.21
  230.4 3.2 collective-permute-done.19
  234.1 1.9 collective-permute-done.21
  236.2 1.6 collective-permute-start.28
  237.8 1.5 collective-permute-start.30
  240.8 9.4 %shard_map.259 = (bf16[4,224,384]{2,1,0:T(8,128)(2,1)}, bf16[4,224,384]{2,1,0:T(8,128)(2,1)}, bf16[4,224,384]{2,1,0:T(8,128)(2,1)}, bf16[4,224,384]{2,1,0:T(8,12...) custom-call(s32[3]{0:T(128)S(1)} %pad_add_fusion.info, ...), custom_call_target="tpu_custom_call" | custom-call | flops 2717908992 | bytes 5505024 | tf_op jit(solution)/shard_map/pallas_call | solution.py:659
  250.8 3.4 collective-permute-start.23
  254.4 1.0 collective-permute-start.44
  255.5 12.2 %collective-permute-done.53 = bf16[4,224,384]{2,1,0:T(8,128)(2,1)S(1)} collective-permute-done((bf16[4,224,384]{2,1,0:T(8,128)(2,1)}, bf16[4,224,384]{2,1,0:T(8,128)(2,1)S(1)}, u32[]{:S(2)}, u32[]{:S(2)}) %collective-permute-start.53) | collective-permute-done | bytes 688160 | tf_op jit(solution)/shard_map/ppermute | solution.py:541
  267.9 3.5 collective-permute-start.32
  272.0 1.2 collective-permute-start.54
  273.5 1.2 collective-permute-done.32
  275.2 4.0 %collective-permute-done.31 = bf16[80,384]{1,0:T(8,128)(2,1)S(1)} collective-permute-done((bf16[80,384]{1,0:T(8,128)(2,1)S(1)}, bf16[80,384]{1,0:T(8,128)(2,1)S(1)}, u32[]{:S(2)}, u32[]{:S(2)}) %collective-permute-start.31) | collective-permute-done | bytes 61472 | tf_op jit(solution)/shard_map/ppermute | solution.py:538
  279.2 0.9 collective-permute-start.45
  280.2 9.6 %collective-permute-done.52 = bf16[4,224,384]{2,1,0:T(8,128)(2,1)S(1)} collective-permute-done((bf16[4,224,384]{2,1,0:T(8,128)(2,1)S(1)}, bf16[4,224,384]{2,1,0:T(8,128)(2,1)S(1)}, u32[]{:S(2)}, u32[]{:S(2)}) %collective-permute-start.52) | collective-permute-done | bytes 688160 | tf_op jit(solution)/shard_map/ppermute | solution.py:541
  290.7 1.0 collective-permute-start.57
  291.7 11.2 %collective-permute-done.43 = bf16[4,224,384]{2,1,0:T(8,128)(2,1)S(1)} collective-permute-done((bf16[4,224,384]{2,1,0:T(8,128)(2,1)S(1)}, bf16[4,224,384]{2,1,0:T(8,128)(2,1)S(1)}, u32[]{:S(2)}, u32[]{:S(2)}) %collective-permute-start.43) | collective-permute-done | bytes 688160 | tf_op jit(solution)/shard_map/ppermute | solution.py:541
  303.3 2.1 collective-permute-start.55
  305.7 1.8 collective-permute-start.48
  307.5 8.7 %collective-permute-done.56 = bf16[224,384]{1,0:T(8,128)(2,1)S(1)} collective-permute-done((bf16[224,384]{1,0:T(8,128)(2,1)S(1)}, bf16[224,384]{1,0:T(8,128)(2,1)S(1)}, u32[]{:S(2)}, u32[]{:S(2)}) %collective-permute-start.56) | collective-permute-done | bytes 172064 | tf_op jit(solution)/shard_map/ppermute | solution.py:538
  316.2 6.4 %collective-permute-start.46 = (bf16[224,384]{1,0:T(8,128)(2,1)S(1)}, bf16[224,384]{1,0:T(8,128)(2,1)S(1)}, u32[]{:S(2)}, u32[]{:S(2)}) collective-permute-start(bf16[224,384]{1,0:T(8,128)(2,1)S(1)} %get-tuple-element.173), channel_id=1, source_target_pairs={{0,2},{1,3},{2,4},{3,5},{4,6},{5,7},{6,0},{7,1},{8,10},{9,11},{10,... | collective-permute-start | bytes 516104 | tf_op jit(solution)/shard_map/ppermute | solution.py:538
  322.7 1.6 collective-permute-start.26
  324.3 4.5 %collective-permute-done.47 = bf16[224,384]{1,0:T(8,128)(2,1)S(1)} collective-permute-done((bf16[224,384]{1,0:T(8,128)(2,1)S(1)}, bf16[224,384]{1,0:T(8,128)(2,1)S(1)}, u32[]{:S(2)}, u32[]{:S(2)}) %collective-permute-start.47) | collective-permute-done | bytes 172064 | tf_op jit(solution)/shard_map/ppermute | solution.py:538
  329.4 1.4 collective-permute-start.49
  330.8 1.6 collective-permute-start.27
  333.0 5.7 %collective-permute-done.27.rest_3_ = bf16[80,384]{1,0:T(8,128)(2,1)S(1)} collective-permute-done((bf16[80,384]{1,0:T(8,128)(2,1)S(1)}, bf16[80,384]{1,0:T(8,128)(2,1)S(1)}, u32[]{:S(2)}, u32[]{:S(2)}) %collective-permute-start.27) | collective-permute-done | bytes 61472 | tf_op jit(solution)/shard_map/ppermute | solution.py:541
  340.4 1.5 collective-permute-start.37
  342.6 1.0 collective-permute-done.36.rest_6_
  344.2 1.1 collective-permute-start.50
  346.3 1.5 collective-permute-start.51
  347.8 1.5 collective-permute-start.59
  349.8 1.5 collective-permute-start.61
  355.4 1.5 shard_map.258
  357.0 3.1 shard_map.257
  360.1 2.2 shard_map.260
  (210 shorter events, 25.6 us)
Async XLA Ops:
  0.7 46.6 %collective-permute-start.4 = (bf16[256,768]{1,0:T(8,128)(2,1)}, bf16[256,768]{1,0:T(8,128)(2,1)S(1)}, u32[]{:S(2)}, u32[]{:S(2)}) collective-permute-start(bf16[256,768]{1,0:T(8,128)(2,1)} %bitcast.69), channel_id=1, source_target_pairs={{0,2},{1,3},{2,4},{3,5},{4,6},{5,7},{6,0},{7,1},{8,10},{9,11},{10,... | collective-permute-start | bytes 1179656 | tf_op jit(solution)/shard_map/ppermute | solution.py:538
  3.7 43.9 %collective-permute-start = (bf16[256,768]{1,0:T(8,128)(2,1)}, bf16[256,768]{1,0:T(8,128)(2,1)S(1)}, u32[]{:S(2)}, u32[]{:S(2)}) collective-permute-start(bf16[256,768]{1,0:T(8,128)(2,1)} %bitcast.70), channel_id=1, source_target_pairs={{0,6},{1,7},{2,0},{3,1},{4,2},{5,3},{6,4},{7,5},{8,14},{9,15},{10,... | collective-permute-start | bytes 1179656 | tf_op jit(solution)/shard_map/ppermute | solution.py:538
  5.8 42.0 %collective-permute-start.2 = (bf16[256,768]{1,0:T(8,128)(2,1)}, bf16[256,768]{1,0:T(8,128)(2,1)S(1)}, u32[]{:S(2)}, u32[]{:S(2)}) collective-permute-start(bf16[256,768]{1,0:T(8,128)(2,1)} %bitcast.71), channel_id=1, source_target_pairs={{0,4},{1,5},{2,6},{3,7},{4,0},{5,1},{6,2},{7,3},{8,12},{9,13},{10,... | collective-permute-start | bytes 1179656 | tf_op jit(solution)/shard_map/ppermute | solution.py:538
  6.8 44.0 %collective-permute-start.6 = (bf16[256,768]{1,0:T(8,128)(2,1)}, bf16[256,768]{1,0:T(8,128)(2,1)S(1)}, u32[]{:S(2)}, u32[]{:S(2)}) collective-permute-start(bf16[256,768]{1,0:T(8,128)(2,1)} %bitcast.72), channel_id=1, source_target_pairs={{0,1},{1,0},{2,3},{3,2},{4,5},{5,4},{6,7},{7,6},{8,9},{9,8},{10,11... | collective-permute-start | bytes 1179656 | tf_op jit(solution)/shard_map/ppermute | solution.py:534
  47.3 8.0 %collective-permute-start.5 = (bf16[256,768]{1,0:T(8,128)(2,1)S(1)}, bf16[256,768]{1,0:T(8,128)(2,1)S(1)}, u32[]{:S(2)}, u32[]{:S(2)}) collective-permute-start(bf16[256,768]{1,0:T(8,128)(2,1)S(1)} %collective-permute-done.4.xa), channel_id=1, source_target_pairs={{0,1},{1,0},{2,3},{3,2},{4,5},{5,4},{6,7},{7,6},{8,9},{9,8},{10,11... | collective-permute-start | bytes 1179656 | tf_op jit(solution)/shard_map/ppermute | solution.py:534
  47.7 16.2 %collective-permute-start.1 = (bf16[256,768]{1,0:T(8,128)(2,1)S(1)}, bf16[256,768]{1,0:T(8,128)(2,1)S(1)}, u32[]{:S(2)}, u32[]{:S(2)}) collective-permute-start(bf16[256,768]{1,0:T(8,128)(2,1)S(1)} %collective-permute-done.xa), channel_id=1, source_target_pairs={{0,1},{1,0},{2,3},{3,2},{4,5},{5,4},{6,7},{7,6},{8,9},{9,8},{10,11... | collective-permute-start | bytes 1179656 | tf_op jit(solution)/shard_map/ppermute | solution.py:534
  47.8 11.8 %collective-permute-start.3 = (bf16[256,768]{1,0:T(8,128)(2,1)S(1)}, bf16[256,768]{1,0:T(8,128)(2,1)S(1)}, u32[]{:S(2)}, u32[]{:S(2)}) collective-permute-start(bf16[256,768]{1,0:T(8,128)(2,1)S(1)} %collective-permute-done.2.xa), channel_id=1, source_target_pairs={{0,1},{1,0},{2,3},{3,2},{4,5},{5,4},{6,7},{7,6},{8,9},{9,8},{10,11... | collective-permute-start | bytes 1179656 | tf_op jit(solution)/shard_map/ppermute | solution.py:534
  97.7 66.0 %copy-start.7 = (bf16[3,256,256]{2,1,0:T(8,128)(2,1)}, bf16[3,256,256]{2,1,0:T(8,128)(2,1)S(1)}, u32[]{:S(2)}) copy-start(bf16[3,256,256]{2,1,0:T(8,128)(2,1)S(1)} %get-tuple-element.124.rm) | copy-start | bytes 1179652
  97.7 1.8 collective-permute-start.7
  113.8 122.2 %copy-start.23 = (bf16[256,768]{1,0:T(8,128)(2,1)}, bf16[256,768]{1,0:T(8,128)(2,1)S(1)}, u32[]{:S(2)}) copy-start(bf16[256,768]{1,0:T(8,128)(2,1)S(1)} %get-tuple-element.156.da_mine) | copy-start | bytes 1179652
  113.8 1.5 collective-permute-start.8
  116.5 62.1 %collective-permute-start.9 = (bf16[512,384]{1,0:T(8,128)(2,1)S(1)}, bf16[512,384]{1,0:T(8,128)(2,1)S(1)}, u32[]{:S(2)}, u32[]{:S(2)}) collective-permute-start(bf16[512,384]{1,0:T(8,128)(2,1)S(1)} %get-tuple-element.130.datt.rest_0_), channel_id=1, source_target_pairs={{0,2},{1,3},{2,4},{3,5},{4,6},{5,7},{6,0},{7,1},{8,10},{9,11},{10,... | collective-permute-start | bytes 1179656 | tf_op jit(solution)/shard_map/ppermute | solution.py:538
  116.9 61.7 %collective-permute-start.10 = (bf16[512,384]{1,0:T(8,128)(2,1)S(1)}, bf16[512,384]{1,0:T(8,128)(2,1)S(1)}, u32[]{:S(2)}, u32[]{:S(2)}) collective-permute-start(bf16[512,384]{1,0:T(8,128)(2,1)S(1)} %get-tuple-element.130.datt.rest_0_), channel_id=1, source_target_pairs={{0,4},{1,5},{2,6},{3,7},{4,0},{5,1},{6,2},{7,3},{8,12},{9,13},{10,... | collective-permute-start | bytes 1179656 | tf_op jit(solution)/shard_map/ppermute | solution.py:538
  119.3 59.3 %collective-permute-start.11 = (bf16[512,384]{1,0:T(8,128)(2,1)S(1)}, bf16[512,384]{1,0:T(8,128)(2,1)S(1)}, u32[]{:S(2)}, u32[]{:S(2)}) collective-permute-start(bf16[512,384]{1,0:T(8,128)(2,1)S(1)} %get-tuple-element.130.datt.rest_0_), channel_id=1, source_target_pairs={{0,6},{1,7},{2,0},{3,1},{4,2},{5,3},{6,4},{7,5},{8,14},{9,15},{10,... | collective-permute-start | bytes 1179656 | tf_op jit(solution)/shard_map/ppermute | solution.py:538
  120.4 27.8 %collective-permute-start.12 = (f32[3,8,512]{2,1,0:T(8,128)S(1)}, f32[3,8,512]{2,1,0:T(8,128)S(1)}, u32[]{:S(2)}, u32[]{:S(2)}) collective-permute-start(f32[3,8,512]{2,1,0:T(8,128)S(1)} %get-tuple-element.132.rest_4_), channel_id=1, source_target_pairs={{0,2},{1,3},{2,4},{3,5},{4,6},{5,7},{6,0},{7,1},{8,10},{9,11},{10,... | collective-permute-start | bytes 147464 | tf_op jit(solution)/shard_map/ppermute | solution.py:538
  121.4 36.4 %collective-permute-start.13 = (f32[3,8,512]{2,1,0:T(8,128)S(1)}, f32[3,8,512]{2,1,0:T(8,128)S(1)}, u32[]{:S(2)}, u32[]{:S(2)}) collective-permute-start(f32[3,8,512]{2,1,0:T(8,128)S(1)} %get-tuple-element.132.rest_4_), channel_id=1, source_target_pairs={{0,4},{1,5},{2,6},{3,7},{4,0},{5,1},{6,2},{7,3},{8,12},{9,13},{10,... | collective-permute-start | bytes 147464 | tf_op jit(solution)/shard_map/ppermute | solution.py:538
  148.2 9.7 %collective-permute-start.14 = (f32[3,8,512]{2,1,0:T(8,128)S(1)}, f32[3,8,512]{2,1,0:T(8,128)S(1)}, u32[]{:S(2)}, u32[]{:S(2)}) collective-permute-start(f32[3,8,512]{2,1,0:T(8,128)S(1)} %get-tuple-element.132.rest_4_), channel_id=1, source_target_pairs={{0,6},{1,7},{2,0},{3,1},{4,2},{5,3},{6,4},{7,5},{8,14},{9,15},{10,... | collective-permute-start | bytes 147464 | tf_op jit(solution)/shard_map/ppermute | solution.py:538
  157.7 5.9 %collective-permute-start.15 = (f32[3,8,512]{2,1,0:T(8,128)S(1)}, f32[3,8,512]{2,1,0:T(8,128)S(1)}, u32[]{:S(2)}, u32[]{:S(2)}) collective-permute-start(f32[3,8,512]{2,1,0:T(8,128)S(1)} %get-tuple-element.133.rest_8_), channel_id=1, source_target_pairs={{0,2},{1,3},{2,4},{3,5},{4,6},{5,7},{6,0},{7,1},{8,10},{9,11},{10,... | collective-permute-start | bytes 147464 | tf_op jit(solution)/shard_map/ppermute | solution.py:538
  157.8 20.8 %collective-permute-start.16 = (f32[3,8,512]{2,1,0:T(8,128)S(1)}, f32[3,8,512]{2,1,0:T(8,128)S(1)}, u32[]{:S(2)}, u32[]{:S(2)}) collective-permute-start(f32[3,8,512]{2,1,0:T(8,128)S(1)} %get-tuple-element.133.rest_8_), channel_id=1, source_target_pairs={{0,4},{1,5},{2,6},{3,7},{4,0},{5,1},{6,2},{7,3},{8,12},{9,13},{10,... | collective-permute-start | bytes 147464 | tf_op jit(solution)/shard_map/ppermute | solution.py:538
  163.7 14.9 %collective-permute-start.17 = (f32[3,8,512]{2,1,0:T(8,128)S(1)}, f32[3,8,512]{2,1,0:T(8,128)S(1)}, u32[]{:S(2)}, u32[]{:S(2)}) collective-permute-start(f32[3,8,512]{2,1,0:T(8,128)S(1)} %get-tuple-element.133.rest_8_), channel_id=1, source_target_pairs={{0,6},{1,7},{2,0},{3,1},{4,2},{5,3},{6,4},{7,5},{8,14},{9,15},{10,... | collective-permute-start | bytes 147464 | tf_op jit(solution)/shard_map/ppermute | solution.py:538
  178.6 60.7 %collective-permute-start.40 = (bf16[256,3072]{1,0:T(8,128)(2,1)S(1)}, bf16[256,3072]{1,0:T(8,128)(2,1)S(1)}, u32[]{:S(2)}, u32[]{:S(2)}) collective-permute-start(bf16[256,3072]{1,0:T(8,128)(2,1)S(1)} %copy-done.35), channel_id=1, source_target_pairs={{0,1},{1,0},{2,3},{3,2},{4,5},{5,4},{6,7},{7,6},{8,9},{9,8},{10,11... | collective-permute-start | bytes 4718600 | tf_op jit(solution)/shard_map/ppermute | solution.py:534
  220.0 8.8 %collective-permute-start.20 = (bf16[4,80,384]{2,1,0:T(8,128)(2,1)S(1)}, bf16[4,80,384]{2,1,0:T(8,128)(2,1)S(1)}, u32[]{:S(2)}, u32[]{:S(2)}) collective-permute-start(bf16[4,80,384]{2,1,0:T(8,128)(2,1)S(1)} %get-tuple-element.143), channel_id=1, source_target_pairs={{0,8},{8,0},{16,24},{24,16},{1,9},{9,1},{17,25},{25,17},{2,10},{10... | collective-permute-start | bytes 737288 | tf_op jit(solution)/shard_map/ppermute | solution.py:541
  221.4 17.9 %collective-permute-start.39 = (bf16[4,256,384]{2,1,0:T(8,128)(2,1)S(1)}, bf16[4,256,384]{2,1,0:T(8,128)(2,1)S(1)}, u32[]{:S(2)}, u32[]{:S(2)}) collective-permute-start(bf16[4,256,384]{2,1,0:T(8,128)(2,1)S(1)} %copy-done.38), channel_id=1, source_target_pairs={{0,1},{1,0},{2,3},{3,2},{4,5},{5,4},{6,7},{7,6},{8,9},{9,8},{10,11... | collective-permute-start | bytes 2359304 | tf_op jit(solution)/shard_map/ppermute | solution.py:534
  221.7 11.9 %collective-permute-start.19 = (bf16[4,80,384]{2,1,0:T(8,128)(2,1)S(1)}, bf16[4,80,384]{2,1,0:T(8,128)(2,1)S(1)}, u32[]{:S(2)}, u32[]{:S(2)}) collective-permute-start(bf16[4,80,384]{2,1,0:T(8,128)(2,1)S(1)} %get-tuple-element.141), channel_id=1, source_target_pairs={{0,8},{8,0},{16,24},{24,16},{1,9},{9,1},{17,25},{25,17},{2,10},{10... | collective-permute-start | bytes 737288 | tf_op jit(solution)/shard_map/ppermute | solution.py:541
  222.2 11.4 %collective-permute-start.29 = (bf16[4,80,384]{2,1,0:T(8,128)(2,1)S(1)}, bf16[4,80,384]{2,1,0:T(8,128)(2,1)S(1)}, u32[]{:S(2)}, u32[]{:S(2)}) collective-permute-start(bf16[4,80,384]{2,1,0:T(8,128)(2,1)S(1)} %get-tuple-element.147), channel_id=1, source_target_pairs={{0,16},{8,24},{16,0},{24,8},{1,17},{9,25},{17,1},{25,9},{2,18},{10... | collective-permute-start | bytes 737288 | tf_op jit(solution)/shard_map/ppermute | solution.py:541
  228.8 7.3 %collective-permute-start.21 = (bf16[4,80,384]{2,1,0:T(8,128)(2,1)S(1)}, bf16[4,80,384]{2,1,0:T(8,128)(2,1)S(1)}, u32[]{:S(2)}, u32[]{:S(2)}) collective-permute-start(bf16[4,80,384]{2,1,0:T(8,128)(2,1)S(1)} %add_convert_fusion.10), channel_id=1, source_target_pairs={{0,16},{8,24},{16,0},{24,8},{1,17},{9,25},{17,1},{25,9},{2,18},{10... | collective-permute-start | bytes 737288 | tf_op jit(solution)/shard_map/ppermute | solution.py:541
  233.6 2.6 collective-permute-start.41
  233.6 4.2 %collective-permute-start.38 = (bf16[256,768]{1,0:T(8,128)(2,1)S(1)}, bf16[256,768]{1,0:T(8,128)(2,1)S(1)}, u32[]{:S(2)}, u32[]{:S(2)}) collective-permute-start(bf16[256,768]{1,0:T(8,128)(2,1)S(1)} %get-tuple-element.152.n_mine), channel_id=1, source_target_pairs={{0,1},{1,0},{2,3},{3,2},{4,5},{5,4},{6,7},{7,6},{8,9},{9,8},{10,11... | collective-permute-start | bytes 1179656 | tf_op jit(solution)/shard_map/ppermute | solution.py:534
  236.0 3.3 collective-permute-start.42
  236.2 18.1 %collective-permute-start.28 = (bf16[4,80,384]{2,1,0:T(8,128)(2,1)S(1)}, bf16[4,80,384]{2,1,0:T(8,128)(2,1)S(1)}, u32[]{:S(2)}, u32[]{:S(2)}) collective-permute-start(bf16[4,80,384]{2,1,0:T(8,128)(2,1)S(1)} %get-tuple-element.145), channel_id=1, source_target_pairs={{0,16},{8,24},{16,0},{24,8},{1,17},{9,25},{17,1},{25,9},{2,18},{10... | collective-permute-start | bytes 737288 | tf_op jit(solution)/shard_map/ppermute | solution.py:541
  237.8 16.5 %collective-permute-start.30 = (bf16[4,80,384]{2,1,0:T(8,128)(2,1)S(1)}, bf16[4,80,384]{2,1,0:T(8,128)(2,1)S(1)}, u32[]{:S(2)}, u32[]{:S(2)}) collective-permute-start(bf16[4,80,384]{2,1,0:T(8,128)(2,1)S(1)} %add_convert_fusion.7), channel_id=1, source_target_pairs={{0,8},{8,0},{16,24},{24,16},{1,9},{9,1},{17,25},{25,17},{2,10},{10... | collective-permute-start | bytes 737288 | tf_op jit(solution)/shard_map/ppermute | solution.py:541
  250.3 17.4 %collective-permute-start.53 = (bf16[4,224,384]{2,1,0:T(8,128)(2,1)}, bf16[4,224,384]{2,1,0:T(8,128)(2,1)S(1)}, u32[]{:S(2)}, u32[]{:S(2)}) collective-permute-start(bf16[4,224,384]{2,1,0:T(8,128)(2,1)} %get-tuple-element.165), channel_id=1, source_target_pairs={{0,16},{8,24},{16,0},{24,8},{1,17},{9,25},{17,1},{25,9},{2,18},{10... | collective-permute-start | bytes 2064392 | tf_op jit(solution)/shard_map/ppermute | solution.py:541
  250.8 17.1 %collective-permute-start.24 = (bf16[80,384]{1,0:T(8,128)(2,1)S(1)}, bf16[80,384]{1,0:T(8,128)(2,1)S(1)}, u32[]{:S(2)}, u32[]{:S(2)}) collective-permute-start(bf16[80,384]{1,0:T(8,128)(2,1)S(1)} %get-tuple-element.180), channel_id=1, source_target_pairs={{0,6},{1,7},{2,0},{3,1},{4,2},{5,3},{6,4},{7,5},{8,14},{9,15},{10,... | collective-permute-start | bytes 184328 | tf_op jit(solution)/shard_map/ppermute | solution.py:538
  250.8 20.6 %collective-permute-start.23 = (bf16[80,384]{1,0:T(8,128)(2,1)S(1)}, bf16[80,384]{1,0:T(8,128)(2,1)S(1)}, u32[]{:S(2)}, u32[]{:S(2)}) collective-permute-start(bf16[80,384]{1,0:T(8,128)(2,1)S(1)} %get-tuple-element.181), channel_id=1, source_target_pairs={{0,4},{1,5},{2,6},{3,7},{4,0},{5,1},{6,2},{7,3},{8,12},{9,13},{10,... | collective-permute-start | bytes 184328 | tf_op jit(solution)/shard_map/ppermute | solution.py:538
  254.3 17.7 %collective-permute-start.22 = (bf16[80,384]{1,0:T(8,128)(2,1)S(1)}, bf16[80,384]{1,0:T(8,128)(2,1)S(1)}, u32[]{:S(2)}, u32[]{:S(2)}) collective-permute-start(bf16[80,384]{1,0:T(8,128)(2,1)S(1)} %get-tuple-element.179), channel_id=1, source_target_pairs={{0,2},{1,3},{2,4},{3,5},{4,6},{5,7},{6,0},{7,1},{8,10},{9,11},{10,... | collective-permute-start | bytes 184328 | tf_op jit(solution)/shard_map/ppermute | solution.py:538
  254.4 18.7 %collective-permute-start.44 = (bf16[4,224,384]{2,1,0:T(8,128)(2,1)}, bf16[4,224,384]{2,1,0:T(8,128)(2,1)S(1)}, u32[]{:S(2)}, u32[]{:S(2)}) collective-permute-start(bf16[4,224,384]{2,1,0:T(8,128)(2,1)} %get-tuple-element.161), channel_id=1, source_target_pairs={{0,8},{8,0},{16,24},{24,16},{1,9},{9,1},{17,25},{25,17},{2,10},{10... | collective-permute-start | bytes 2064392 | tf_op jit(solution)/shard_map/ppermute | solution.py:541
  267.7 5.7 %collective-permute-start.33 = (bf16[80,384]{1,0:T(8,128)(2,1)S(1)}, bf16[80,384]{1,0:T(8,128)(2,1)S(1)}, u32[]{:S(2)}, u32[]{:S(2)}) collective-permute-start(bf16[80,384]{1,0:T(8,128)(2,1)S(1)} %get-tuple-element.177), channel_id=1, source_target_pairs={{0,6},{1,7},{2,0},{3,1},{4,2},{5,3},{6,4},{7,5},{8,14},{9,15},{10,... | collective-permute-start | bytes 184328 | tf_op jit(solution)/shard_map/ppermute | solution.py:538
  267.9 6.8 %collective-permute-start.32 = (bf16[80,384]{1,0:T(8,128)(2,1)S(1)}, bf16[80,384]{1,0:T(8,128)(2,1)S(1)}, u32[]{:S(2)}, u32[]{:S(2)}) collective-permute-start(bf16[80,384]{1,0:T(8,128)(2,1)S(1)} %get-tuple-element.178), channel_id=1, source_target_pairs={{0,4},{1,5},{2,6},{3,7},{4,0},{5,1},{6,2},{7,3},{8,12},{9,13},{10,... | collective-permute-start | bytes 184328 | tf_op jit(solution)/shard_map/ppermute | solution.py:538
  271.4 18.4 %collective-permute-start.52 = (bf16[4,224,384]{2,1,0:T(8,128)(2,1)S(1)}, bf16[4,224,384]{2,1,0:T(8,128)(2,1)S(1)}, u32[]{:S(2)}, u32[]{:S(2)}) collective-permute-start(bf16[4,224,384]{2,1,0:T(8,128)(2,1)S(1)} %copy-done.41), channel_id=1, source_target_pairs={{0,16},{8,24},{16,0},{24,8},{1,17},{9,25},{17,1},{25,9},{2,18},{10... | collective-permute-start | bytes 2064392 | tf_op jit(solution)/shard_map/ppermute | solution.py:541
  272.0 18.4 %collective-permute-start.54 = (bf16[4,224,384]{2,1,0:T(8,128)(2,1)S(1)}, bf16[4,224,384]{2,1,0:T(8,128)(2,1)S(1)}, u32[]{:S(2)}, u32[]{:S(2)}) collective-permute-start(bf16[4,224,384]{2,1,0:T(8,128)(2,1)S(1)} %add_convert_fusion.1), channel_id=1, source_target_pairs={{0,8},{8,0},{16,24},{24,16},{1,9},{9,1},{17,25},{25,17},{2,10},{10... | collective-permute-start | bytes 2064392 | tf_op jit(solution)/shard_map/ppermute | solution.py:541
  273.2 6.1 %collective-permute-start.31 = (bf16[80,384]{1,0:T(8,128)(2,1)S(1)}, bf16[80,384]{1,0:T(8,128)(2,1)S(1)}, u32[]{:S(2)}, u32[]{:S(2)}) collective-permute-start(bf16[80,384]{1,0:T(8,128)(2,1)S(1)} %get-tuple-element.176), channel_id=1, source_target_pairs={{0,2},{1,3},{2,4},{3,5},{4,6},{5,7},{6,0},{7,1},{8,10},{9,11},{10,... | collective-permute-start | bytes 184328 | tf_op jit(solution)/shard_map/ppermute | solution.py:538
  273.4 75.9 %collective-permute-start.18 = (f32[256,768]{1,0:T(8,128)S(1)}, f32[256,768]{1,0:T(8,128)S(1)}, u32[]{:S(2)}, u32[]{:S(2)}) collective-permute-start(f32[256,768]{1,0:T(8,128)S(1)} %copy-done.37), channel_id=1, source_target_pairs={{0,1},{1,0},{2,3},{3,2},{4,5},{5,4},{6,7},{7,6},{8,9},{9,8},{10,11... | collective-permute-start | bytes 2359304 | tf_op jit(solution)/shard_map/ppermute | solution.py:534
  274.7 28.2 %collective-permute-start.43 = (bf16[4,224,384]{2,1,0:T(8,128)(2,1)S(1)}, bf16[4,224,384]{2,1,0:T(8,128)(2,1)S(1)}, u32[]{:S(2)}, u32[]{:S(2)}) collective-permute-start(bf16[4,224,384]{2,1,0:T(8,128)(2,1)S(1)} %copy-done.40), channel_id=1, source_target_pairs={{0,8},{8,0},{16,24},{24,16},{1,9},{9,1},{17,25},{25,17},{2,10},{10... | collective-permute-start | bytes 2064392 | tf_op jit(solution)/shard_map/ppermute | solution.py:541
  279.2 24.0 %collective-permute-start.45 = (bf16[4,224,384]{2,1,0:T(8,128)(2,1)S(1)}, bf16[4,224,384]{2,1,0:T(8,128)(2,1)S(1)}, u32[]{:S(2)}, u32[]{:S(2)}) collective-permute-start(bf16[4,224,384]{2,1,0:T(8,128)(2,1)S(1)} %add_convert_fusion.4), channel_id=1, source_target_pairs={{0,16},{8,24},{16,0},{24,8},{1,17},{9,25},{17,1},{25,9},{2,18},{10... | collective-permute-start | bytes 2064392 | tf_op jit(solution)/shard_map/ppermute | solution.py:541
  289.8 39.6 %collective-permute-start.25 = (bf16[80,384]{1,0:T(8,128)(2,1)S(1)}, bf16[80,384]{1,0:T(8,128)(2,1)S(1)}, u32[]{:S(2)}, u32[]{:S(2)}) collective-permute-start(bf16[80,384]{1,0:T(8,128)(2,1)S(1)} %fusion.11.rest_0_), channel_id=1, source_target_pairs={{0,8},{8,0},{16,24},{24,16},{1,9},{9,1},{17,25},{25,17},{2,10},{10... | collective-permute-start | bytes 184328 | tf_op jit(solution)/shard_map/ppermute | solution.py:541
  290.7 15.0 %collective-permute-start.57 = (bf16[224,384]{1,0:T(8,128)(2,1)S(1)}, bf16[224,384]{1,0:T(8,128)(2,1)S(1)}, u32[]{:S(2)}, u32[]{:S(2)}) collective-permute-start(bf16[224,384]{1,0:T(8,128)(2,1)S(1)} %get-tuple-element.171), channel_id=1, source_target_pairs={{0,6},{1,7},{2,0},{3,1},{4,2},{5,3},{6,4},{7,5},{8,14},{9,15},{10,... | collective-permute-start | bytes 516104 | tf_op jit(solution)/shard_map/ppermute | solution.py:538
  302.9 13.3 %collective-permute-start.56 = (bf16[224,384]{1,0:T(8,128)(2,1)S(1)}, bf16[224,384]{1,0:T(8,128)(2,1)S(1)}, u32[]{:S(2)}, u32[]{:S(2)}) collective-permute-start(bf16[224,384]{1,0:T(8,128)(2,1)S(1)} %get-tuple-element.172), channel_id=1, source_target_pairs={{0,4},{1,5},{2,6},{3,7},{4,0},{5,1},{6,2},{7,3},{8,12},{9,13},{10,... | collective-permute-start | bytes 516104 | tf_op jit(solution)/shard_map/ppermute | solution.py:538
  303.3 12.9 %collective-permute-start.55 = (bf16[224,384]{1,0:T(8,128)(2,1)S(1)}, bf16[224,384]{1,0:T(8,128)(2,1)S(1)}, u32[]{:S(2)}, u32[]{:S(2)}) collective-permute-start(bf16[224,384]{1,0:T(8,128)(2,1)S(1)} %get-tuple-element.170), channel_id=1, source_target_pairs={{0,2},{1,3},{2,4},{3,5},{4,6},{5,7},{6,0},{7,1},{8,10},{9,11},{10,... | collective-permute-start | bytes 516104 | tf_op jit(solution)/shard_map/ppermute | solution.py:538
  305.7 17.0 %collective-permute-start.48 = (bf16[224,384]{1,0:T(8,128)(2,1)S(1)}, bf16[224,384]{1,0:T(8,128)(2,1)S(1)}, u32[]{:S(2)}, u32[]{:S(2)}) collective-permute-start(bf16[224,384]{1,0:T(8,128)(2,1)S(1)} %get-tuple-element.174), channel_id=1, source_target_pairs={{0,6},{1,7},{2,0},{3,1},{4,2},{5,3},{6,4},{7,5},{8,14},{9,15},{10,... | collective-permute-start | bytes 516104 | tf_op jit(solution)/shard_map/ppermute | solution.py:538
  316.2 12.6 %collective-permute-start.47 = (bf16[224,384]{1,0:T(8,128)(2,1)S(1)}, bf16[224,384]{1,0:T(8,128)(2,1)S(1)}, u32[]{:S(2)}, u32[]{:S(2)}) collective-permute-start(bf16[224,384]{1,0:T(8,128)(2,1)S(1)} %get-tuple-element.175), channel_id=1, source_target_pairs={{0,4},{1,5},{2,6},{3,7},{4,0},{5,1},{6,2},{7,3},{8,12},{9,13},{10,... | collective-permute-start | bytes 516104 | tf_op jit(solution)/shard_map/ppermute | solution.py:538
  316.2 12.6 %collective-permute-start.46 = (bf16[224,384]{1,0:T(8,128)(2,1)S(1)}, bf16[224,384]{1,0:T(8,128)(2,1)S(1)}, u32[]{:S(2)}, u32[]{:S(2)}) collective-permute-start(bf16[224,384]{1,0:T(8,128)(2,1)S(1)} %get-tuple-element.173), channel_id=1, source_target_pairs={{0,2},{1,3},{2,4},{3,5},{4,6},{5,7},{6,0},{7,1},{8,10},{9,11},{10,... | collective-permute-start | bytes 516104 | tf_op jit(solution)/shard_map/ppermute | solution.py:538
  322.7 8.1 %collective-permute-start.26 = (bf16[80,384]{1,0:T(8,128)(2,1)S(1)}, bf16[80,384]{1,0:T(8,128)(2,1)S(1)}, u32[]{:S(2)}, u32[]{:S(2)}) collective-permute-start(bf16[80,384]{1,0:T(8,128)(2,1)S(1)} %fusion.11.rest_0_), channel_id=1, source_target_pairs={{0,16},{8,24},{16,0},{24,8},{1,17},{9,25},{17,1},{25,9},{2,18},{10... | collective-permute-start | bytes 184328 | tf_op jit(solution)/shard_map/ppermute | solution.py:541
  328.8 3.7 %collective-permute-start.34 = (bf16[80,384]{1,0:T(8,128)(2,1)S(1)}, bf16[80,384]{1,0:T(8,128)(2,1)S(1)}, u32[]{:S(2)}, u32[]{:S(2)}) collective-permute-start(bf16[80,384]{1,0:T(8,128)(2,1)S(1)} %fusion.8), channel_id=1, source_target_pairs={{0,1},{1,0},{2,3},{3,2},{4,5},{5,4},{6,7},{7,6},{8,9},{9,8},{10,11... | collective-permute-start | bytes 184328 | tf_op jit(solution)/shard_map/ppermute | solution.py:534
  328.8 19.0 %collective-permute-start.58 = (bf16[224,384]{1,0:T(8,128)(2,1)S(1)}, bf16[224,384]{1,0:T(8,128)(2,1)S(1)}, u32[]{:S(2)}, u32[]{:S(2)}) collective-permute-start(bf16[224,384]{1,0:T(8,128)(2,1)S(1)} %fusion.2), channel_id=1, source_target_pairs={{0,1},{1,0},{2,3},{3,2},{4,5},{5,4},{6,7},{7,6},{8,9},{9,8},{10,11... | collective-permute-start | bytes 516104 | tf_op jit(solution)/shard_map/ppermute | solution.py:534
  329.4 20.4 %collective-permute-start.49 = (bf16[224,384]{1,0:T(8,128)(2,1)S(1)}, bf16[224,384]{1,0:T(8,128)(2,1)S(1)}, u32[]{:S(2)}, u32[]{:S(2)}) collective-permute-start(bf16[224,384]{1,0:T(8,128)(2,1)S(1)} %fusion.5.rest_0_), channel_id=1, source_target_pairs={{0,8},{8,0},{16,24},{24,16},{1,9},{9,1},{17,25},{25,17},{2,10},{10... | collective-permute-start | bytes 516104 | tf_op jit(solution)/shard_map/ppermute | solution.py:541
  330.8 7.9 %collective-permute-start.27 = (bf16[80,384]{1,0:T(8,128)(2,1)S(1)}, bf16[80,384]{1,0:T(8,128)(2,1)S(1)}, u32[]{:S(2)}, u32[]{:S(2)}) collective-permute-start(bf16[80,384]{1,0:T(8,128)(2,1)S(1)} %fusion.11.rest_0_), channel_id=1, source_target_pairs={{0,24},{8,16},{16,8},{24,0},{1,25},{9,17},{17,9},{25,1},{2,26},{10... | collective-permute-start | bytes 184328 | tf_op jit(solution)/shard_map/ppermute | solution.py:541
  332.5 7.3 %collective-permute-start.35 = (bf16[80,384]{1,0:T(8,128)(2,1)S(1)}, bf16[80,384]{1,0:T(8,128)(2,1)S(1)}, u32[]{:S(2)}, u32[]{:S(2)}) collective-permute-start(bf16[80,384]{1,0:T(8,128)(2,1)S(1)} %collective-permute-done.34.rest_4_), channel_id=1, source_target_pairs={{0,8},{8,0},{16,24},{24,16},{1,9},{9,1},{17,25},{25,17},{2,10},{10... | collective-permute-start | bytes 184328 | tf_op jit(solution)/shard_map/ppermute | solution.py:541
  339.3 4.2 %collective-permute-start.36 = (bf16[80,384]{1,0:T(8,128)(2,1)S(1)}, bf16[80,384]{1,0:T(8,128)(2,1)S(1)}, u32[]{:S(2)}, u32[]{:S(2)}) collective-permute-start(bf16[80,384]{1,0:T(8,128)(2,1)S(1)} %collective-permute-done.34.rest_4_), channel_id=1, source_target_pairs={{0,16},{8,24},{16,0},{24,8},{1,17},{9,25},{17,1},{25,9},{2,18},{10... | collective-permute-start | bytes 184328 | tf_op jit(solution)/shard_map/ppermute | solution.py:541
  340.4 5.2 %collective-permute-start.37 = (bf16[80,384]{1,0:T(8,128)(2,1)S(1)}, bf16[80,384]{1,0:T(8,128)(2,1)S(1)}, u32[]{:S(2)}, u32[]{:S(2)}) collective-permute-start(bf16[80,384]{1,0:T(8,128)(2,1)S(1)} %collective-permute-done.34.rest_4_), channel_id=1, source_target_pairs={{0,24},{8,16},{16,8},{24,0},{1,25},{9,17},{17,9},{25,1},{2,26},{10... | collective-permute-start | bytes 184328 | tf_op jit(solution)/shard_map/ppermute | solution.py:541
  344.2 15.9 %collective-permute-start.50 = (bf16[224,384]{1,0:T(8,128)(2,1)S(1)}, bf16[224,384]{1,0:T(8,128)(2,1)S(1)}, u32[]{:S(2)}, u32[]{:S(2)}) collective-permute-start(bf16[224,384]{1,0:T(8,128)(2,1)S(1)} %fusion.5.rest_0_), channel_id=1, source_target_pairs={{0,16},{8,24},{16,0},{24,8},{1,17},{9,25},{17,1},{25,9},{2,18},{10... | collective-permute-start | bytes 516104 | tf_op jit(solution)/shard_map/ppermute | solution.py:541
  346.3 13.8 %collective-permute-start.51 = (bf16[224,384]{1,0:T(8,128)(2,1)S(1)}, bf16[224,384]{1,0:T(8,128)(2,1)S(1)}, u32[]{:S(2)}, u32[]{:S(2)}) collective-permute-start(bf16[224,384]{1,0:T(8,128)(2,1)S(1)} %fusion.5.rest_0_), channel_id=1, source_target_pairs={{0,24},{8,16},{16,8},{24,0},{1,25},{9,17},{17,9},{25,1},{2,26},{10... | collective-permute-start | bytes 516104 | tf_op jit(solution)/shard_map/ppermute | solution.py:541
  347.8 12.3 %collective-permute-start.59 = (bf16[224,384]{1,0:T(8,128)(2,1)S(1)}, bf16[224,384]{1,0:T(8,128)(2,1)S(1)}, u32[]{:S(2)}, u32[]{:S(2)}) collective-permute-start(bf16[224,384]{1,0:T(8,128)(2,1)S(1)} %collective-permute-done.58.rest_4_), channel_id=1, source_target_pairs={{0,8},{8,0},{16,24},{24,16},{1,9},{9,1},{17,25},{25,17},{2,10},{10... | collective-permute-start | bytes 516104 | tf_op jit(solution)/shard_map/ppermute | solution.py:541
  349.3 10.8 %collective-permute-start.60 = (bf16[224,384]{1,0:T(8,128)(2,1)S(1)}, bf16[224,384]{1,0:T(8,128)(2,1)S(1)}, u32[]{:S(2)}, u32[]{:S(2)}) collective-permute-start(bf16[224,384]{1,0:T(8,128)(2,1)S(1)} %collective-permute-done.58.rest_4_), channel_id=1, source_target_pairs={{0,16},{8,24},{16,0},{24,8},{1,17},{9,25},{17,1},{25,9},{2,18},{10... | collective-permute-start | bytes 516104 | tf_op jit(solution)/shard_map/ppermute | solution.py:541
  349.8 10.3 %collective-permute-start.61 = (bf16[224,384]{1,0:T(8,128)(2,1)S(1)}, bf16[224,384]{1,0:T(8,128)(2,1)S(1)}, u32[]{:S(2)}, u32[]{:S(2)}) collective-permute-start(bf16[224,384]{1,0:T(8,128)(2,1)S(1)} %collective-permute-done.58.rest_4_), channel_id=1, source_target_pairs={{0,24},{8,16},{16,8},{24,0},{1,25},{9,17},{17,9},{25,1},{2,26},{10... | collective-permute-start | bytes 516104 | tf_op jit(solution)/shard_map/ppermute | solution.py:541
  (45 other events, 523.8 us)
